TPU v7x, 512 devices: a whole 4x8x8 slice. The times are simulated.
512 devices in a mesh: seq: 16 (over y, core), table: 32 (over z, x).
Axes of the slice: x: 4, y: 8, z: 8, core: 2. Of those that a mesh axis runs over, the one named last changes fastest.
Arguments:
- table: bfloat16 [32768, 512], P('table'), may hold values from -6 to 6
- item_rows: int32 [32, 2048], P('table', 'seq'), may hold values from 0 to 32767, as said below
- lengths: int32 [32], P('table'), may hold values from 512 to 2048, as said below
- w_in: bfloat16 [512, 2048], replicated, may hold values from -0.25 to 0.25
- w_out: bfloat16 [512, 512], replicated, may hold values from -0.25 to 0.25
- cotangent: bfloat16 [32, 2048, 512], P('table', 'seq'), may hold values from -6 to 6
Outputs:
- table_grad: float32 [32768, 512], P('table', 'seq')
- w_out_grad: float32 [512, 512], P('table')
Inputs may be any that keep to these rules, and one draw needn't show every extreme that they name: `item_rows`: A row's owner is its index divided by 1024. The 128 events of one device name rows of at most 8 events for each owner; in every draw one owner gets exactly 8 events from every device of a group along table. `lengths`: in every draw some user's history is live in all 2048 positions.
All inputs are finite; a program needn't handle non-finite values.
Results may differ from a plain program's by a relative error of at most 0.025.
Values may be sent and summed in bfloat16 or wider, within the bound.
A program may use at most 128 MiB of HBM per device.

v0:
```python
import jax
import jax.numpy as jnp
from jax import lax
from jax.sharding import PartitionSpec as P

HEADS = 8


EPS = 1e-05


def positions(index, events, seq_count):
    block = index // events
    within = index % events
    half = events // 2
    span = jnp.where(within < half, block, 2 * seq_count - 1 - block)
    return span * half + within % half


def normalize(values):
    center = values - jnp.mean(values, axis=-1, keepdims=True)
    scale_inv = lax.rsqrt(jnp.mean(center * center, axis=-1, keepdims=True) + EPS)
    return (center * scale_inv, scale_inv)


def norm_back(grad, normed, scale_inv):
    first = jnp.mean(grad, axis=-1, keepdims=True)
    second = jnp.mean(grad * normed, axis=-1, keepdims=True)
    return scale_inv * (grad - first - normed * second)


def silu_slope(values):
    sigma = jax.nn.sigmoid(values)
    return sigma * (1.0 + values * (1.0 - sigma))


def on_device(table, item_rows, lengths, w_in, w_out, cotangent):
    events = item_rows.shape[1]
    width = w_out.shape[0]
    table_rows = table.shape[0]
    seq_count = lax.axis_size("seq")
    owners = lax.axis_size("table")
    capacity = 2 * events // owners
    head_size = width // HEADS
    factor = head_size ** (-0.5)
    seq_place = lax.axis_index("seq")
    row_ids = item_rows[0]
    length = lengths[0]
    counter = jnp.arange(events, dtype=jnp.int32)
    query_pos = positions(seq_place * events + counter, events, seq_count)
    is_live = query_pos < length
    owner_of = row_ids // table_rows
    local_row = row_ids % table_rows
    same_owner = (owner_of[:, None] == owner_of[None, :]) & (counter[None, :] < counter[:, None])
    slot_rank = jnp.sum(same_owner.astype(jnp.int32), axis=1)
    slot_index = owner_of * capacity + slot_rank
    chosen = slot_index[:, None] == jnp.arange(owners * capacity, dtype=jnp.int32)[None, :]
    slot_used = jnp.any(chosen, axis=0)
    source_row = jnp.sum(jnp.where(chosen, counter[:, None], 0), axis=0)
    requested = jnp.sum(jnp.where(chosen, local_row[:, None], 0), axis=0).reshape(owners, capacity)
    wanted = lax.all_to_all(requested, "table", split_axis=0, concat_axis=0, tiled=True)
    fetched = table[wanted]
    returned = lax.all_to_all(fetched, "table", split_axis=0, concat_axis=0, tiled=True)
    embedded = returned.reshape(owners * capacity, width)[slot_index]
    normed_f, inv_first = normalize(embedded.astype(jnp.float32))
    normed = normed_f.astype(jnp.bfloat16)
    before = jnp.dot(normed, w_in, preferred_element_type=jnp.float32)
    projected = jax.nn.silu(before).astype(jnp.bfloat16)
    gate_u = projected[:, :width]
    value_loc = projected[:, width : 2 * width]
    query_loc = projected[:, 2 * width : 3 * width]
    key_loc = projected[:, 3 * width :]
    query_heads = query_loc.reshape(events, HEADS, head_size)
    key_heads = key_loc.reshape(events, HEADS, head_size)
    value_heads = value_loc.reshape(events, HEADS, head_size)
    key_piece = lax.all_gather(key_loc, "seq", axis=0, tiled=True)
    value_piece = lax.all_gather(value_loc, "seq", axis=0, tiled=True)
    count = key_piece.shape[0]
    key_pos = positions(jnp.arange(count, dtype=jnp.int32), events, seq_count)
    visible = (key_pos[None, :] <= query_pos[:, None]) & (key_pos < length)[None, :]
    score = (
        jnp.einsum(
            "qhd,khd->hqk",
            query_heads,
            key_piece.reshape(count, HEADS, head_size),
            preferred_element_type=jnp.float32,
        )
        * factor
    )
    weight = jnp.where(visible[None], jax.nn.silu(score), 0.0).astype(jnp.bfloat16)
    output = jnp.einsum(
        "hqk,khd->qhd",
        weight,
        value_piece.reshape(count, HEADS, head_size),
        preferred_element_type=jnp.float32,
    )
    attended = output.reshape(events, width)
    normed_y, inv_second = normalize(attended)
    mixed = (normed_y * gate_u.astype(jnp.float32)).astype(jnp.bfloat16)
    grad = jnp.where(is_live[:, None], cotangent[0], jnp.zeros_like(cotangent[0]))
    weight_term = lax.dot_general(
        mixed, grad, (((0,), (0,)), ((), ())), preferred_element_type=jnp.float32
    )
    weight_part = lax.psum_scatter(
        weight_term.astype(jnp.bfloat16), "table", scatter_dimension=0, tiled=True
    )
    w_out_grad = lax.psum(weight_part, "seq").astype(jnp.float32)
    grad_mixed = lax.dot_general(
        grad, w_out, (((1,), (1,)), ((), ())), preferred_element_type=jnp.float32
    )
    grad_gate = grad_mixed * normed_y
    grad_attended = norm_back(grad_mixed * gate_u.astype(jnp.float32), normed_y, inv_second).astype(
        jnp.bfloat16
    )
    grad_heads = grad_attended.reshape(events, HEADS, head_size)
    key_piece = lax.all_gather(key_loc, "seq", axis=0, tiled=True)
    value_piece = lax.all_gather(value_loc, "seq", axis=0, tiled=True)
    count = key_piece.shape[0]
    key_pos = positions(jnp.arange(count, dtype=jnp.int32), events, seq_count)
    visible = (key_pos[None, :] <= query_pos[:, None]) & (key_pos < length)[None, :]
    key_split = key_piece.reshape(count, HEADS, head_size)
    score = (
        jnp.einsum("qhd,khd->hqk", query_heads, key_split, preferred_element_type=jnp.float32)
        * factor
    )
    grad_weight = jnp.einsum(
        "qhd,khd->hqk",
        grad_heads,
        value_piece.reshape(count, HEADS, head_size),
        preferred_element_type=jnp.float32,
    )
    grad_score = jnp.where(visible[None], grad_weight * silu_slope(score), 0.0).astype(jnp.bfloat16)
    grad_query = jnp.einsum(
        "hqk,khd->qhd", grad_score, key_split, preferred_element_type=jnp.float32
    )
    grad_q = factor * grad_query.reshape(events, width)
    query_piece = lax.all_gather(query_loc, "seq", axis=0, tiled=True)
    grad_piece = lax.all_gather(grad_attended, "seq", axis=0, tiled=True)
    count = query_piece.shape[0]
    remote_pos = positions(jnp.arange(count, dtype=jnp.int32), events, seq_count)
    visible = (query_pos[None, :] <= remote_pos[:, None]) & is_live[None, :]
    query_split = query_piece.reshape(count, HEADS, head_size)
    grad_split = grad_piece.reshape(count, HEADS, head_size)
    score = (
        jnp.einsum("qhd,khd->hqk", query_split, key_heads, preferred_element_type=jnp.float32)
        * factor
    )
    weight = jnp.where(visible[None], jax.nn.silu(score), 0.0).astype(jnp.bfloat16)
    grad_value = jnp.einsum("hqk,qhd->khd", weight, grad_split, preferred_element_type=jnp.float32)
    grad_weight = jnp.einsum(
        "qhd,khd->hqk", grad_split, value_heads, preferred_element_type=jnp.float32
    )
    grad_score = jnp.where(visible[None], grad_weight * silu_slope(score), 0.0).astype(jnp.bfloat16)
    grad_key = jnp.einsum(
        "hqk,qhd->khd", grad_score, query_split, preferred_element_type=jnp.float32
    )
    grad_k = factor * grad_key.reshape(events, width)
    grad_v = grad_value.reshape(events, width)
    grad_proj = jnp.concatenate([grad_gate, grad_v, grad_q, grad_k], axis=1)
    grad_before = (grad_proj * silu_slope(before)).astype(jnp.bfloat16)
    grad_normed = lax.dot_general(
        grad_before, w_in, (((1,), (1,)), ((), ())), preferred_element_type=jnp.float32
    )
    grad_rows = grad.astype(jnp.float32) + norm_back(grad_normed, normed_f, inv_first)
    outgoing = jnp.where(slot_used[:, None], grad_rows[source_row], 0.0).reshape(
        owners, capacity, width
    )
    arrived = lax.all_to_all(
        outgoing.astype(jnp.bfloat16), "table", split_axis=0, concat_axis=0, tiled=True
    ).astype(outgoing.dtype)
    dense = jax.ops.segment_sum(
        arrived.reshape(-1, width), wanted.reshape(-1), num_segments=table_rows
    )
    table_grad = lax.psum_scatter(
        dense.astype(jnp.bfloat16), "seq", scatter_dimension=1, tiled=True
    ).astype(jnp.float32)
    return (table_grad, w_out_grad)


def solution(mesh):
    return jax.shard_map(
        on_device,
        mesh=mesh,
        in_specs=(
            P("table", None),
            P("table", "seq"),
            P("table"),
            P(),
            P(),
            P("table", "seq", None),
        ),
        out_specs=(P("table", "seq"), P("table", None)),
        check_vma=False,
    )
```

profile of v0, /device:TPU:1, one launch (start us, length us, event | category | flops | bytes accessed | tf_op | source)
XLA Modules:
  0.0 511.7 jit_solution(14298300899382668682)
XLA Ops:
  7.2 0.8 fusion.53
  9.0 22.1 %all_to_all.22 = s32[32,1,8]{2,1,0:T(1,128)S(1)} all-to-all(s32[32,1,8]{2,1,0:T(1,128)S(1)} %bitcast.124), channel_id=1, replica_groups=mesh['seq'=16,'table'=32] {'table'}, dimensions={0} | all-to-all | bytes 2048 | tf_op jit(solution)/shard_map/all_to_all | solution.py:61
  31.3 3.3 gather_fusion
  34.5 3.9 all-to-all-start.1
  38.4 0.7 fusion.52
  39.1 9.8 %all-to-all-done.1 = bf16[32,8,512]{2,1,0:T(8,128)(2,1)S(1)} async-done(((bf16[32,8,512]{2,1,0:T(8,128)(2,1)}), bf16[32,8,512]{2,1,0:T(8,128)(2,1)S(1)}, u32[]{:S(2)}, u32[]{:S(2)}) %all-to-all-start.1) | async-done | bytes 262176 | tf_op jit(solution)/shard_map/all_to_all | solution.py:63
  49.0 0.8 gather_fusion.1
  50.2 1.5 multiply_convert_fusion
  51.7 0.7 fusion.70
  52.5 0.7 all-gather.7.cloned.1.call-update
  54.3 1.1 copy.50
  55.5 37.4 %all-gather.5.cloned.1.call-done = bf16[2048,512]{1,0:T(8,128)(2,1)} async-done(((bf16[128,512]{1,0:T(8,128)(2,1)}), bf16[2048,512]{1,0:T(8,128)(2,1)}) %all-gather.5.cloned.1.call-update) | async-done | bytes 2097168 | tf_op jit(solution)/shard_map/all_gather | solution.py:77
  92.9 4.0 copy.49
  96.8 39.0 %all-gather.7.cloned.1.call-done = bf16[2048,512]{1,0:T(8,128)(2,1)} async-done(((bf16[128,512]{1,0:T(8,128)(2,1)}), bf16[2048,512]{1,0:T(8,128)(2,1)}) %all-gather.7.cloned.1.call-update) | async-done | bytes 2097168 | tf_op jit(solution)/shard_map/all_gather | solution.py:76
  135.8 3.9 copy.51
  139.8 3.0 fusion.72
  142.9 3.4 fusion.71
  146.3 1.1 copy.52
  147.4 1.0 fusion.26
  148.5 1.5 fusion.37
  150.0 0.9 fusion.27
  151.2 0.7 broadcast_in_dim.115
  152.5 1.1 compare_and_fusion
  153.8 1.0 copy.56
  154.9 10.5 %fusion.5 = f32[8,64,128]{2,1,0:T(8,128)} fusion(bf16[2048,8,64]{0,2,1:T(8,128)(2,1)} %bitcast.105, f32[8,128,2048]{2,1,0:T(8,128)} %copy-done.1, bf16[128,8,64]{0,2,1:T(8,128)(2,1)S(1)} %bitcast.122, bf16[2048,8,64]{0,2,1:T(8,128)(2,1)} %bitcast.110, pred[128,2048]{1,0:T(8,128)(4,1)} %copy-done.6), kind=kOutput, calls=%fused_computation.16 | convolution fusion | flops 560005120 | bytes 13238272 | tf_op jit(solution)/shard_map/hqk,khd->qhd/dot_general | solution.py:133
  165.3 1.8 copy.59
  167.1 1.9 convolution_convert_fusion
  169.1 9.8 %all-gather.11.cloned.1.call-done = bf16[2048,512]{1,0:T(8,128)(2,1)} async-done(((bf16[128,512]{1,0:T(8,128)(2,1)}), bf16[2048,512]{1,0:T(8,128)(2,1)}) %all-gather.11.cloned.1.call-update) | async-done | bytes 2097168 | tf_op jit(solution)/shard_map/all_gather | solution.py:137
  178.9 4.0 copy.54
  182.9 6.3 %fusion.73 = f32[8,2048,128]{2,1,0:T(8,128)} fusion(bf16[2048,8,64]{0,2,1:T(8,128)(2,1)} %bitcast.106, bf16[128,8,64]{0,2,1:T(8,128)(2,1)S(1)} %bitcast.115), kind=kOutput, calls=%fused_computation.152 | convolution fusion | flops 268435456 | bytes 10616832 | tf_op jit(solution)/shard_map/qhd,khd->hqk/dot_general | solution.py:145
  189.1 32.5 %all-gather.9.cloned.1.call-done = bf16[2048,512]{1,0:T(8,128)(2,1)} async-done(((bf16[128,512]{1,0:T(8,128)(2,1)}), bf16[2048,512]{1,0:T(8,128)(2,1)}) %all-gather.9.cloned.1.call-update) | async-done | bytes 2097168 | tf_op jit(solution)/shard_map/all_gather | solution.py:138
  221.6 4.0 copy.53
  225.6 6.6 %fusion.1 = f32[8,64,128]{2,1,0:T(8,128)S(1)} fusion(bf16[2048,8,64]{0,2,1:T(8,128)(2,1)} %bitcast.112, f32[8,2048,128]{2,1,0:T(8,128)} %fusion.73, pred[2048,128]{1,0:T(8,128)(4,1)S(1)} %copy-done.8), kind=kOutput, calls=%fused_computation.11 | convolution fusion | flops 283115520 | bytes 11010048 | tf_op jit(solution)/shard_map/hqk,qhd->khd/dot_general | solution.py:149
  232.2 9.4 %fusion.4 = f32[8,64,128]{2,1,0:T(8,128)S(1)} fusion(bf16[2048,8,64]{0,2,1:T(8,128)(2,1)} %bitcast.107, f32[8,2048,128]{2,1,0:T(8,128)} %fusion.73, bf16[2048,8,64]{0,2,1:T(8,128)(2,1)} %bitcast.113, bf16[128,8,64]{0,2,1:T(8,128)(2,1)S(1)} %bitcast.121, pred[2048,128]{1,0:T(8,128)(4,1)S(1)} %copy-done.8), kind=kOutput, calls=%fused_computation.15 | convolution fusion | flops 560005120 | bytes 13238272 | tf_op jit(solution)/shard_map/hqk,qhd->khd/dot_general | solution.py:154
  241.9 2.2 fusion.69
  244.3 1.3 gather_fusion.2
  245.6 0.8 fusion.10
  246.4 9.9 %all-to-all-start.2 = ((bf16[32,8,512]{2,1,0:T(8,128)(2,1)}), bf16[32,8,512]{2,1,0:T(8,128)(2,1)S(1)}, u32[]{:S(2)}, u32[]{:S(2)}) async-start(bf16[32,8,512]{2,1,0:T(8,128)(2,1)} %fusion.10), calls=%async_computation.2 | async-start | bytes 524288 | tf_op jit(solution)/shard_map/all_to_all | solution.py:168
  257.1 0.7 reduce.6
  257.9 10.3 %all-to-all-done.2 = bf16[32,8,512]{2,1,0:T(8,128)(2,1)S(1)} async-done(((bf16[32,8,512]{2,1,0:T(8,128)(2,1)}), bf16[32,8,512]{2,1,0:T(8,128)(2,1)S(1)}, u32[]{:S(2)}, u32[]{:S(2)}) %all-to-all-start.2) | async-done | bytes 262176 | tf_op jit(solution)/shard_map/all_to_all | solution.py:168
  268.2 3.5 scatter_custom_fusion
  271.8 1.7 convert_element_type.69
  273.5 1.3 copy.62
  274.9 164.2 %reduce-scatter.5.cloned.1.call-done = bf16[16,512]{1,0:T(8,128)(2,1)} async-done(((bf16[512,512]{1,0:T(8,128)(2,1)}), bf16[16,512]{1,0:T(8,128)(2,1)}) %reduce-scatter.5.cloned.1.call-update) | async-done | bytes 16400 | tf_op jit(solution)/shard_map/reduce_scatter | solution.py:104
  439.1 48.1 %psum.7 = bf16[16,512]{1,0:T(8,128)(2,1)S(1)} all-reduce(bf16[16,512]{1,0:T(8,128)(2,1)} %reduce-scatter.5.cloned.1.call-done), channel_id=1, replica_groups=mesh['seq'=16,'table'=32] {'seq'}, use_global_device_ids=true, to_apply=%region_15.16 | all-reduce | flops 8192 | bytes 32768 | tf_op jit(solution)/shard_map/psum | solution.py:107
  487.8 15.2 %reduce-scatter.7.cloned.1.call-done = bf16[32,1024]{1,0:T(8,128)(2,1)} async-done(((bf16[512,1024]{1,0:T(8,128)(2,1)}), bf16[32,1024]{1,0:T(8,128)(2,1)}) %reduce-scatter.7.cloned.1.call-update) | async-done | bytes 65552
  503.1 1.0 copy.63
  504.1 0.8 copy.61
  (81 shorter events, 5.2 us)
Async XLA Ops:
  7.2 43.0 %copy-start = (bf16[512,2048]{1,0:T(8,128)(2,1)S(1)}, bf16[512,2048]{1,0:T(8,128)(2,1)}, u32[]{:S(2)}) copy-start(bf16[512,2048]{1,0:T(8,128)(2,1)} %param.9) | copy-start | bytes 6291460
  34.5 14.5 %all-to-all-start.1 = ((bf16[32,8,512]{2,1,0:T(8,128)(2,1)}), bf16[32,8,512]{2,1,0:T(8,128)(2,1)S(1)}, u32[]{:S(2)}, u32[]{:S(2)}) async-start(bf16[32,8,512]{2,1,0:T(8,128)(2,1)} %bitcast.6), calls=%async_computation.1 | async-start | bytes 524288 | tf_op jit(solution)/shard_map/all_to_all | solution.py:63
  38.4 54.5 %all-gather.5.cloned.1.call-start = ((), (), s32[]{:S(2)}) async-start(), calls=%async_computation.5 | async-start | bytes 2228224 | tf_op jit(solution)/shard_map/all_gather | solution.py:77
  49.9 4.1 copy-start.14
  50.2 3.9 copy-start.16
  52.4 83.4 %all-gather.7.cloned.1.call-start = ((), (), s32[]{:S(2)}) async-start(), calls=%async_computation.6 | async-start | bytes 2228224 | tf_op jit(solution)/shard_map/all_gather | solution.py:76
  53.2 125.7 %all-gather.11.cloned.1.call-start = ((), (), s32[]{:S(2)}) async-start(), calls=%async_computation.8 | async-start | bytes 2228224 | tf_op jit(solution)/shard_map/all_gather | solution.py:137
  54.0 167.7 %all-gather.9.cloned.1.call-start = ((), (), s32[]{:S(2)}) async-start(), calls=%async_computation.7 | async-start | bytes 2228224 | tf_op jit(solution)/shard_map/all_gather | solution.py:138
  54.1 98.4 %copy-start.11 = (pred[128]{0:T(512)(128)(4,1)}, pred[128]{0:T(512)(128)(4,1)S(1)}, u32[]{:S(2)}) copy-start(pred[128]{0:T(512)(128)(4,1)S(1)} %broadcast_compare_fusion.1) | copy-start | bytes 388
  54.3 88.5 %copy-start.6 = (pred[128,2048]{1,0:T(8,128)(4,1)}, pred[128,2048]{1,0:T(8,128)(4,1)S(1)}, u32[]{:S(2)}) copy-start(pred[128,2048]{1,0:T(8,128)(4,1)S(1)} %compare_and_fusion.1) | copy-start | bytes 786436
  139.8 3.1 copy-start.2
  142.8 3.5 copy-start.1
  142.8 5.6 %copy-start.3 = (bf16[1,128,512]{2,1,0:T(8,128)(2,1)S(1)}, bf16[1,128,512]{2,1,0:T(8,128)(2,1)}, u32[]{:S(2)}) copy-start(bf16[1,128,512]{2,1,0:T(8,128)(2,1)} %param.11) | copy-start | bytes 393220
  142.8 10.7 %copy-start.5 = (bf16[128,512]{1,0:T(8,128)(2,1)S(1)}, bf16[128,512]{1,0:T(8,128)(2,1)}, u32[]{:S(2)}) copy-start(bf16[128,512]{1,0:T(8,128)(2,1)} %get-tuple-element.16) | copy-start | bytes 393220
  142.9 10.8 %copy-start.4 = (bf16[128,512]{1,0:T(8,128)(2,1)S(1)}, bf16[128,512]{1,0:T(8,128)(2,1)}, u32[]{:S(2)}) copy-start(bf16[128,512]{1,0:T(8,128)(2,1)} %get-tuple-element.17) | copy-start | bytes 393220
  147.4 3.4 copy-start.10
  148.5 2.4 copy-start.13
  150.9 288.3 %reduce-scatter.5.cloned.1.call-start = ((), (), s32[]{:S(2)}) async-start(), calls=%async_computation.9 | async-start | bytes 540672 | tf_op jit(solution)/shard_map/reduce_scatter | solution.py:104
  182.8 42.7 %copy-start.8 = (pred[2048,128]{1,0:T(8,128)(4,1)S(1)}, pred[2048,128]{1,0:T(8,128)(4,1)}, u32[]{:S(2)}) copy-start(pred[2048,128]{1,0:T(8,128)(4,1)} %compare_and_fusion) | copy-start | bytes 786436
  232.2 9.7 %copy-start.7 = (f32[128,512]{1,0:T(8,128)S(1)}, f32[128,512]{1,0:T(8,128)}, u32[]{:S(2)}) copy-start(f32[128,512]{1,0:T(8,128)} %copy.59) | copy-start | bytes 786436
  241.6 2.5 copy-start.12
  241.6 2.5 copy-start.15
  241.6 2.5 copy-start.17
  241.6 4.0 copy-start.9
  246.4 21.8 %all-to-all-start.2 = ((bf16[32,8,512]{2,1,0:T(8,128)(2,1)}), bf16[32,8,512]{2,1,0:T(8,128)(2,1)S(1)}, u32[]{:S(2)}, u32[]{:S(2)}) async-start(bf16[32,8,512]{2,1,0:T(8,128)(2,1)} %fusion.10), calls=%async_computation.2 | async-start | bytes 524288 | tf_op jit(solution)/shard_map/all_to_all | solution.py:168
  256.4 246.7 %reduce-scatter.7.cloned.1.call-start = ((), (), s32[]{:S(2)}) async-start(), calls=%async_computation.10 | async-start | bytes 1114112
Sparse Core Ops, SparseCore 0:
  52.6 40.2 all-gather.4
  95.0 40.7 all-gather.6
  138.0 40.8 all-gather.10
  180.9 40.7 all-gather.8
  225.9 213.2 reduce-scatter.4
  442.0 60.9 reduce-scatter.6
where the time goes:
time: 514 us; the launch traced here: 512 us
  waiting for transfers between devices  319 us (62%)
  blocking collectives  70.2 us (14%)
  matrix products  46.3 us (9%)
  local copies, waits for them, and re-layouts  32.1 us (6%)
  between operations  15.2 us (3%)
  starting transfers between devices  14.4 us (3%)
  other arithmetic  14.3 us (3%)
    reduce_scatter x1, waiting for transfers between devices, on_device(): lax.psum_scatter(weight_term.astype(jnp.bfloat16), 'table', scatter_dimen...  164 us
    psum x1, blocking collectives, on_device(): w_out_grad = lax.psum(weight_part, 'seq').astype(jnp.float32)  48.1 us
    all_gather x1, waiting for transfers between devices, on_device(): key_piece = lax.all_gather(key_loc, 'seq', axis=0, tiled=True)  39 us
    all_gather x1, waiting for transfers between devices, on_device(): value_piece = lax.all_gather(value_loc, 'seq', axis=0, tiled=True)  37.4 us
    all_gather x1, waiting for transfers between devices, on_device(): grad_piece = lax.all_gather(grad_attended, 'seq', axis=0, tiled=True)  32.5 us
    all_to_all x1, blocking collectives, on_device(): lax.all_to_all(requested, 'table', split_axis=0, concat_axis=0, tiled=True)  22.1 us
    unnamed x7, waiting for transfers between devices  16 us
    dot_general x1, matrix products, on_device(): jnp.einsum('hqk,khd->qhd', grad_score, key_split, preferred_element_type=...  10.5 us
  transfers between devices with their start and end apart: 8, of which 8 were waited for; matrix products, arithmetic and copies ran while one was open for 16% of the time, Pallas kernels for 0%

commit v1 on v0

v1 whole, which is shorter than its diff:
```python
import jax
import jax.numpy as jnp
from jax import lax
from jax.experimental import pallas as pl
from jax.experimental.pallas import tpu as pltpu
from jax.sharding import PartitionSpec as P

EPS = 1e-05
MESH = pl.DeviceIdType.MESH
F32 = jnp.float32
BF16 = jnp.bfloat16
I32 = jnp.int32

N_SEQ = 16
N_TABLE = 32
EVENTS = 128
WIDTH = 512
HEADS = 8
HEAD = 64
CAP = 8
ROWS_T = 1024
SLOTS = N_TABLE * CAP
HIDDEN = -64.0


def mm(a, b):
    return jnp.dot(a, b, preferred_element_type=F32)


def mm_t(a, b):
    return lax.dot_general(a, b, (((1,), (1,)), ((), ())), preferred_element_type=F32)


def iota(shape, dim):
    return lax.broadcasted_iota(I32, shape, dim)


def one_hot(mask):
    return jnp.where(mask, 1.0, 0.0).astype(BF16)


def swap(tile):
    return pltpu.roll(tile, 64, tile.ndim - 1)


def left(shape):
    return iota(shape, len(shape) - 1) < 64


def kernel(
    rows_ref,
    len_ref,
    cot_ref,
    table_hbm,
    w_in_hbm,
    w_out_hbm,
    out_ref,
    w_grad_ref,
    table_v,
    w_in_v,
    w_out_v,
    ids_send,
    ids_land,
    fetch_send,
    fetch_land,
    slot_send,
    slot_land,
    qkv_send,
    qkv_land,
    kv_sib,
    e_send,
    e_land,
    stat_send,
    stat_land,
    ny_send,
    ny_land,
    w_send,
    w_land,
    part_send,
    part_land,
    sib_send,
    sib_land,
    back_send,
    back_land,
    dx_send,
    dx_land,
    col_send,
    col_land,
    grad_s,
    dz_t,
    u_t,
    nx_s,
    slope_s,
    kv_nat,
    kv_t,
    q_pad,
    dy_pad,
    a_t,
    g_t,
    y_t,
    dq_t,
    dkv_s,
    hot_hi,
    mask_lo,
    load_sem,
    send_sem,
    recv_sem,
    qkv_sem,
):
    me_s = lax.axis_index("seq")
    me_t = lax.axis_index("table")
    y = me_s // 2
    core = me_s % 2
    sibling = me_s + 1 - 2 * core

    loads = [
        pltpu.make_async_copy(src, dst, load_sem.at[k])
        for k, (src, dst) in enumerate(
            ((table_hbm, table_v), (w_out_hbm, w_out_v), (w_in_hbm, w_in_v))
        )
    ]
    for load in loads:
        load.start()

    barrier = pltpu.get_barrier_semaphore()

    def greet_table(d, carry):
        pl.semaphore_signal(
            barrier, inc=1, device_id={"table": (me_t + d) % N_TABLE}, device_id_type=MESH
        )
        return carry

    def greet_seq(d, carry):
        pl.semaphore_signal(
            barrier, inc=1, device_id={"seq": (me_s + d) % N_SEQ}, device_id_type=MESH
        )
        return carry

    lax.fori_loop(1, N_TABLE, greet_table, 0)
    lax.fori_loop(1, N_SEQ, greet_seq, 0)

    def remote(src, dst, k, where, recv=None):
        return pltpu.make_async_remote_copy(
            src_ref=src,
            dst_ref=dst,
            send_sem=send_sem.at[k],
            recv_sem=recv_sem.at[k] if recv is None else recv,
            device_id=where,
            device_id_type=MESH,
        )

    def to_table(src, dst, k, split):
        def body(d, carry):
            peer = (me_t + d) % N_TABLE
            remote(src.at[peer] if split else src, dst.at[me_t], k, {"table": peer}).start()
            return carry

        lax.fori_loop(1, N_TABLE, body, 0)

    def to_seq(src, dst, k, split):
        def body(d, carry):
            peer = (me_s + d) % N_SEQ
            remote(src.at[peer] if split else src, dst.at[me_s], k, {"seq": peer}).start()
            return carry

        lax.fori_loop(1, N_SEQ, body, 0)

    def to_heads(src, dst, k, split, sems=None):
        def body(d, carry):
            peer = (y + d) % HEADS
            recv = None if sems is None else sems.at[y]
            remote(
                src.at[peer] if split else src, dst.at[y], k, {"seq": 2 * peer + core}, recv
            ).start()
            return carry

        lax.fori_loop(1, HEADS, body, 0)

    def wait_recv(ref, k):
        pltpu.make_async_copy(ref, ref, recv_sem.at[k]).wait()

    def wait_sent(ref, k):
        pltpu.make_async_copy(ref, ref, send_sem.at[k]).wait()

    ids_row = rows_ref[...]
    ids_own = jnp.broadcast_to(ids_row, (8, EVENTS))
    ids_send[...] = ids_own
    ids_land[me_t] = ids_own
    pl.semaphore_wait(barrier, N_TABLE - 1 + N_SEQ - 1)
    to_table(ids_send, ids_land, 0, False)

    square = (EVENTS, EVENTS)
    row_of, col_of = iota(square, 0), iota(square, 1)
    ids_wide = jnp.broadcast_to(ids_row, square)
    ids_col = jnp.sum(
        jnp.where(row_of == col_of, ids_wide.astype(F32), 0.0), axis=1, keepdims=True
    ).astype(I32)
    owner_row = ids_wide >> 10
    owner_col = jnp.broadcast_to(ids_col >> 10, square)
    same = owner_row == owner_col
    rank_col = jnp.sum(
        jnp.where(same & (col_of < row_of), 1.0, 0.0), axis=1, keepdims=True
    ).astype(I32)
    rank_row = jnp.sum(
        jnp.where(same & (row_of < col_of), 1.0, 0.0), axis=0, keepdims=True
    ).astype(I32)
    slot_col = (ids_col >> 10) * 16 + rank_col
    slot_row = (ids_row >> 10) * CAP + rank_row

    half = iota((EVENTS, 1), 0)
    span = jnp.where(half < 64, me_s, 2 * N_SEQ - 1 - me_s)
    live = (span * 64 + (half & 63)) < len_ref[0]
    grad = jnp.where(live, cot_ref[...].astype(F32), 0.0)
    grad_b = grad.astype(BF16)
    grad_s[...] = grad
    loads[1].wait()
    dz_t[...] = mm_t(w_out_v[...], grad_b)

    wait_recv(ids_land.at[pl.ds(0, N_TABLE - 1)], 0)
    ids = ids_land[...].reshape(SLOTS, EVENTS)
    mine = (ids >> 10) == me_t
    before = one_hot(row_of < col_of)
    rank = mm(one_hot(mine), before)
    turn = (iota((SLOTS, EVENTS), 0) & 7).astype(F32)
    picked = jnp.where(mine & (rank == turn), (ids & 1023).astype(F32) + 1.0, 0.0)
    asked = jnp.sum(picked, axis=1, keepdims=True) - 1.0
    loads[0].wait()
    hot = one_hot(iota((SLOTS, ROWS_T), 1) == asked.astype(I32))

    def stack_halves(values):
        cut = values.reshape(N_TABLE, CAP, WIDTH)
        return jnp.concatenate([cut[:, :, :256], cut[:, :, 256:]], axis=1).astype(BF16)

    fetch_send[...] = stack_halves(mm(hot, table_v[...]))
    to_table(fetch_send, fetch_land, 1, True)
    fetch_land[me_t] = fetch_send[me_t]

    tiles = []
    for q in range(4):
        piece = asked[64 * q : 64 * q + 64]
        twice = jnp.concatenate([piece, piece], axis=0)
        tiles.append(jnp.broadcast_to(twice, square).T[0:1])
    slots = jnp.concatenate(tiles + tiles, axis=0)
    slot_send[...] = slots
    slot_land[me_s] = slots
    to_seq(slot_send, slot_land, 2, False)

    place = iota((EVENTS, 2 * SLOTS), 1)
    pick_lo = one_hot(place == slot_col)
    pick_hi = one_hot(place == slot_col + CAP)
    loads[2].wait()
    wait_recv(fetch_land.at[pl.ds(0, N_TABLE - 1)], 1)
    fetched = fetch_land[...].reshape(2 * SLOTS, 256)
    emb = jnp.concatenate([mm(pick_lo, fetched), mm(pick_hi, fetched)], axis=1)

    center = emb - jnp.mean(emb, axis=1, keepdims=True)
    rs1 = lax.rsqrt(jnp.mean(center * center, axis=1, keepdims=True) + EPS)
    nx = center * rs1
    nx_s[...] = nx
    normed = nx.astype(BF16)

    def project(k):
        cols = slice(WIDTH * k, WIDTH * k + WIDTH)
        pre = mm(normed, w_in_v[:, cols])
        sigma = 0.5 + 0.5 * jnp.tanh(0.5 * pre)
        slope_s[:, cols] = sigma * (1.0 + pre * (1.0 - sigma))
        return (pre * sigma).astype(BF16).astype(F32)

    values, queries, keys = project(1), project(2) * 0.0625, project(3)
    lane_e = left((EVENTS, 128))
    lane_h = left((HEAD, 128))
    for p in range(4):
        cols = slice(128 * p, 128 * p + 128)
        kt, vt, qt = keys[:, cols], values[:, cols], queries[:, cols]
        q_lo, q_hi = qt[:64], qt[64:]
        qkv_send[2 * p, 0:128] = jnp.where(lane_e, kt, swap(vt)).astype(BF16)
        qkv_send[2 * p + 1, 0:128] = jnp.where(lane_e, swap(kt), vt).astype(BF16)
        qkv_send[2 * p, 128:192] = jnp.where(lane_h, q_lo, swap(q_hi)).astype(BF16)
        qkv_send[2 * p + 1, 128:192] = jnp.where(lane_h, swap(q_lo), q_hi).astype(BF16)
    to_heads(qkv_send, qkv_land, 3, True, qkv_sem)
    qkv_land[y] = qkv_send[y]

    gate = project(0)
    gate_t = gate.T
    u_t[...] = gate_t
    e_full = dz_t[...] * gate_t
    e_full = e_full - jnp.mean(e_full, axis=0, keepdims=True)
    e_send[...] = e_full.reshape(HEADS, HEAD, EVENTS).astype(BF16)
    to_heads(e_send, e_land, 4, True)
    e_land[y] = e_send[y]

    def pass_on(d, carry):
        peer = (y + HEADS - d) % HEADS

        @pl.when(d > 0)
        def _():
            pltpu.make_async_copy(qkv_land.at[peer], qkv_land.at[peer], qkv_sem.at[peer]).wait()

        remote(
            qkv_land.at[peer, pl.ds(0, 128)], kv_sib.at[peer], 5, {"seq": sibling}
        ).start()
        return carry

    lax.fori_loop(0, HEADS, pass_on, 0)

    for i in range(HEADS):
        block = qkv_land[i]
        kv_nat[pl.ds(pl.multiple_of((2 * i + core) * 64, 64), 64)] = block[0:64]
        kv_nat[pl.ds(pl.multiple_of((31 - 2 * i - core) * 64, 64), 64)] = block[64:128]
        packed = block[128:192].astype(F32)
        q_pad[64 * i : 64 * i + 64] = jnp.where(lane_h, packed, 0.0).astype(BF16)
        q_pad[64 * (15 - i) : 64 * (16 - i)] = jnp.where(lane_h, swap(packed), 0.0).astype(BF16)
    wait_recv(kv_sib, 5)
    for i in range(HEADS):
        block = kv_sib[i]
        kv_nat[pl.ds(pl.multiple_of((2 * i + 1 - core) * 64, 64), 64)] = block[0:64]
        kv_nat[pl.ds(pl.multiple_of((30 - 2 * i + core) * 64, 64), 64)] = block[64:128]
    for k in range(4):
        kv_t[k] = kv_nat[512 * k : 512 * k + 512].T

    def forward(t, carry):
        q = q_pad[pl.ds(pl.multiple_of(256 * t, 256), 256)]
        lane = 256 * t + iota((1, 256), 1)
        block_q = lane >> 6
        block_q = 2 * block_q + jnp.where(block_q < 8, core, 1 - core)
        pos_q = block_q * 64 + (lane & 63)

        def inner(k, total):
            index = t * (t + 1) // 2 + k
            kv = kv_nat[pl.ds(pl.multiple_of(512 * k, 512), 512)]
            h = mm_t(kv, q)
            pos_k = 512 * k + iota((512, 1), 0)
            h = jnp.where(pos_k <= pos_q, h, HIDDEN)
            th = jnp.tanh(h)
            a = (h + h * th).astype(BF16)
            a_t[index] = a
            g_t[index] = (1.0 + th) + h * (1.0 - th * th)
            return total + mm(kv_t[k, 64:128], a)

        total = lax.fori_loop(0, t + 1, inner, jnp.zeros((HEAD, 256), F32))
        y_t[2 * t] = total[:, :128]
        y_t[2 * t + 1] = total[:, 128:]
        return carry

    lax.fori_loop(0, 4, forward, 0)

    wait_recv(e_land.at[pl.ds(0, HEADS - 1)], 4)
    e_in = [e_land[i].astype(F32) for i in range(HEADS)]
    e_tiles = []
    for p in range(8):
        if p < 4:
            tile = jnp.where(lane_h, e_in[2 * p], swap(e_in[2 * p + 1]))
        else:
            tile = jnp.where(lane_h, swap(e_in[15 - 2 * p]), e_in[14 - 2 * p])
        e_tiles.append(tile[None])
    e_all = jnp.concatenate(e_tiles, axis=0)
    y_all = y_t[...]
    mean_h = jnp.sum(y_all, axis=1) * (1.0 / HEAD)
    spread = y_all - mean_h[:, None, :]
    stats = jnp.concatenate(
        [mean_h, jnp.sum(spread * spread, axis=1), jnp.sum(e_all * y_all, axis=1)], axis=0
    )
    stat_send[...] = stats
    stat_land[y] = stats
    to_heads(stat_send, stat_land, 6, False)

    wait_recv(slot_land.at[pl.ds(0, N_SEQ - 1)], 2)
    lane_8 = left((8, 128))

    def prepare(pair, carry):
        both = jnp.where(lane_8, slot_land[2 * pair], slot_land[2 * pair + 1]).astype(I32)
        span_rows = pl.ds(pl.multiple_of(128 * pair, 128), 128)
        for q in range(4):
            line = both[q : q + 1]
            hot_hi[q, pair] = one_hot(iota((256, 128), 0) == (line & 255))
            column = jnp.broadcast_to((line >> 8).astype(F32), square).T
            mask_lo[q, span_rows] = jnp.where(
                (col_of >> 5).astype(F32) == column, 1.0, 0.0
            )
        return carry

    lax.fori_loop(0, N_SEQ // 2, prepare, 0)

    wait_recv(stat_land.at[pl.ds(0, HEADS - 1)], 6)
    st = stat_land[...]
    means = st[:, 0:8]
    mean = jnp.sum(means, axis=0) * (1.0 / HEADS)
    off = means - mean[None]
    total = jnp.sum(st[:, 8:16], axis=0) + HEAD * jnp.sum(off * off, axis=0)
    rs2 = lax.rsqrt(total * (1.0 / WIDTH) + EPS)
    lean = rs2 * jnp.sum(st[:, 16:24], axis=0) * (1.0 / WIDTH)
    ny = (y_all - mean[:, None, :]) * rs2[:, None, :]
    dy = rs2[:, None, :] * (e_all - ny * lean[:, None, :])
    for p in range(8):
        tall = jnp.concatenate([jnp.zeros((HEAD, 128), F32), dy[p]], axis=0)
        dy_pad[128 * p : 128 * p + 128] = tall.T.astype(BF16)

    def by_source(tiles, i):
        if i % 2 == 0:
            return jnp.where(lane_h, tiles[i // 2], tiles[(15 - i) // 2])
        return swap(jnp.where(lane_h, tiles[(15 - i) // 2], tiles[i // 2]))

    for i in range(HEADS):
        ny_send[i] = by_source([ny[p] for p in range(8)], i).astype(BF16)
    to_heads(ny_send, ny_land, 7, True)
    ny_land[y] = ny_send[y]

    dq_t[...] = jnp.zeros_like(dq_t)

    def backward(k, carry):
        kv = kv_nat[pl.ds(pl.multiple_of(512 * k, 512), 512)]

        def inner(t, total):
            index = t * (t + 1) // 2 + k
            span_q = pl.ds(pl.multiple_of(256 * t, 256), 256)
            dy_q = dy_pad[span_q]
            ds = (mm_t(kv, dy_q) * g_t[index]).astype(BF16)
            dq_t[t] += mm(kv_t[k, 0:64], ds)
            return total + mm(ds, q_pad[span_q]) + mm(a_t[index], dy_q)

        total = lax.fori_loop(k, 4, inner, jnp.zeros((512, 128), F32))
        dkv_s[pl.ds(pl.multiple_of(512 * k, 512), 512)] = total
        return carry

    lax.fori_loop(0, 4, backward, 0)

    def both_halves(first, second):
        return jnp.concatenate(
            [
                dkv_s[pl.ds(pl.multiple_of(first * 64, 64), 64)],
                dkv_s[pl.ds(pl.multiple_of(second * 64, 64), 64)],
            ],
            axis=0,
        )

    for i in range(HEADS):
        sib_send[i] = both_halves(2 * i + 1 - core, 30 - 2 * i + core).astype(BF16)
    sibling_copy = remote(sib_send, sib_land, 8, {"seq": sibling})
    sibling_copy.start()

    dq_tiles = []
    for t in range(4):
        both = dq_t[t] * 0.0625
        dq_tiles += [both[:, :128], both[:, 128:]]
    for i in range(HEADS):
        back_send[i, 128:192] = by_source(dq_tiles, i).astype(BF16)
    wait_recv(sib_land, 8)
    for i in range(HEADS):
        own = both_halves(2 * i + core, 31 - 2 * i - core) + sib_land[i].astype(F32)
        back_send[i, 0:128] = own.astype(BF16)
    to_heads(back_send, back_land, 9, True)
    back_land[y] = back_send[y]

    wait_recv(ny_land.at[pl.ds(0, HEADS - 1)], 7)
    ny_full = ny_land[...].reshape(WIDTH, EVENTS).astype(F32)
    z_t = (ny_full * u_t[...]).astype(BF16)
    w_send[...] = mm(z_t, grad_s[...].astype(BF16)).reshape(N_TABLE, 16, WIDTH).astype(BF16)
    to_table(w_send, w_land, 10, True)
    w_land[me_t] = w_send[me_t]
    d_u = (dz_t[...] * ny_full).T

    wait_recv(back_land.at[pl.ds(0, HEADS - 1)], 9)
    d_k, d_v, d_q = [], [], []
    for p in range(4):
        first = back_land[2 * p, 0:128].astype(F32)
        second = back_land[2 * p + 1, 0:128].astype(F32)
        d_k.append(jnp.where(lane_e, first, swap(second)))
        d_v.append(jnp.where(lane_e, swap(first), second))
        pair = [back_land[2 * p + n, 128:192].astype(F32) for n in range(2)]
        d_q.append(jnp.concatenate(pair, axis=0).T)
    d_proj = jnp.concatenate([d_u] + d_v + d_q + d_k, axis=1)
    d_pre = (d_proj * slope_s[...]).astype(BF16)
    dn = mm_t(d_pre, w_in_v[...])
    nx = nx_s[...]
    first = jnp.mean(dn, axis=1, keepdims=True)
    second = jnp.mean(dn * nx, axis=1, keepdims=True)
    d_x = grad_s[...] + rs1 * (dn - first - nx * second)

    place_t = one_hot(iota((SLOTS, EVENTS), 0) == slot_row)
    dx_send[...] = stack_halves(mm(place_t, d_x.astype(BF16)))
    to_table(dx_send, dx_land, 11, True)
    dx_land[me_t] = dx_send[me_t]

    wait_recv(w_land.at[pl.ds(0, N_TABLE - 1)], 10)
    part = jnp.sum(w_land[...].astype(F32), axis=0).astype(BF16)
    part_send[...] = part
    part_land[me_s] = part
    to_seq(part_send, part_land, 12, False)

    wait_recv(dx_land.at[pl.ds(0, N_TABLE - 1)], 11)
    group = iota((64, 128), 1) >> 5
    for side in range(2):
        rows = dx_land[:, 8 * side : 8 * side + 8].astype(F32).reshape(SLOTS, 256)
        for tile in range(2):
            cut = rows[:, 128 * tile : 128 * tile + 128]
            turned = [cut] + [pltpu.roll(cut, 32 * r, 1) for r in range(1, 4)]
            for g in range(4):
                chunk = turned[(0 - g) % 4][0:64]
                for q in range(1, 4):
                    chunk = jnp.where(group == q, turned[(q - g) % 4][64 * q : 64 * q + 64], chunk)
                col_send[8 * side + 4 * tile + g] = chunk.astype(BF16)
    to_seq(col_send, col_land, 13, True)
    col_land[me_s] = col_send[me_s]

    wait_recv(part_land.at[pl.ds(0, N_SEQ - 1)], 12)
    w_grad_ref[...] = jnp.sum(part_land[...].astype(F32), axis=0)

    spread_of = iota((128, WIDTH), 1)
    spread_to = one_hot(
        iota((128, WIDTH), 0) == 32 * (spread_of >> 7) + (spread_of & 31)
    )
    wait_recv(col_land.at[pl.ds(0, N_SEQ - 1)], 13)
    wide = mm(col_land[...].reshape(N_SEQ * 64, 128), spread_to)
    total = jnp.zeros((256, 128), F32)
    for q in range(4):
        placed = (wide[:, 128 * q : 128 * q + 128] * mask_lo[q]).astype(BF16)
        hot_q = jnp.concatenate([hot_hi[q, pair] for pair in range(N_SEQ // 2)], axis=1)
        total = total + mm(hot_q, placed)
    out_ref[...] = total

    wait_sent(ids_land.at[pl.ds(0, N_TABLE - 1)], 0)
    wait_sent(fetch_send.at[pl.ds(0, N_TABLE - 1)], 1)
    wait_sent(slot_land.at[pl.ds(0, N_SEQ - 1)], 2)
    wait_sent(qkv_send.at[pl.ds(0, HEADS - 1)], 3)
    wait_sent(e_send.at[pl.ds(0, HEADS - 1)], 4)
    wait_sent(kv_sib, 5)
    wait_sent(stat_land.at[pl.ds(0, HEADS - 1)], 6)
    wait_sent(ny_send.at[pl.ds(0, HEADS - 1)], 7)
    wait_sent(sib_send, 8)
    wait_sent(back_send.at[pl.ds(0, HEADS - 1)], 9)
    wait_sent(w_send.at[pl.ds(0, N_TABLE - 1)], 10)
    wait_sent(dx_send.at[pl.ds(0, N_TABLE - 1)], 11)
    wait_sent(part_land.at[pl.ds(0, N_SEQ - 1)], 12)
    wait_sent(col_send.at[pl.ds(0, N_SEQ - 1)], 13)


def on_device(table, item_rows, lengths, w_in, w_out, cotangent):
    vmem = pl.BlockSpec(memory_space=pltpu.VMEM)
    smem = pl.BlockSpec(memory_space=pltpu.SMEM)
    anywhere = pl.BlockSpec(memory_space=pl.ANY)
    buf = pltpu.VMEM
    scratch = [
        buf((ROWS_T, WIDTH), BF16),
        buf((WIDTH, 4 * WIDTH), BF16),
        buf((WIDTH, WIDTH), BF16),
        buf((8, EVENTS), I32),
        buf((N_TABLE, 8, EVENTS), I32),
        buf((N_TABLE, 16, 256), BF16),
        buf((N_TABLE, 16, 256), BF16),
        buf((8, 128), F32),
        buf((N_SEQ, 8, 128), F32),
        buf((HEADS, 192, 128), BF16),
        buf((HEADS, 192, 128), BF16),
        buf((HEADS, 128, 128), BF16),
        buf((HEADS, HEAD, 128), BF16),
        buf((HEADS, HEAD, 128), BF16),
        buf((24, 128), F32),
        buf((HEADS, 24, 128), F32),
        buf((HEADS, HEAD, 128), BF16),
        buf((HEADS, HEAD, 128), BF16),
        buf((N_TABLE, 16, WIDTH), BF16),
        buf((N_TABLE, 16, WIDTH), BF16),
        buf((16, WIDTH), BF16),
        buf((N_SEQ, 16, WIDTH), BF16),
        buf((HEADS, 128, 128), BF16),
        buf((HEADS, 128, 128), BF16),
        buf((HEADS, 192, 128), BF16),
        buf((HEADS, 192, 128), BF16),
        buf((N_TABLE, 16, 256), BF16),
        buf((N_TABLE, 16, 256), BF16),
        buf((N_SEQ, 64, 128), BF16),
        buf((N_SEQ, 64, 128), BF16),
        buf((EVENTS, WIDTH), F32),
        buf((WIDTH, EVENTS), F32),
        buf((WIDTH, EVENTS), F32),
        buf((EVENTS, WIDTH), F32),
        buf((EVENTS, 4 * WIDTH), F32),
        buf((2048, 128), BF16),
        buf((4, 128, 512), BF16),
        buf((1024, 128), BF16),
        buf((1024, 128), BF16),
        buf((10, 512, 256), BF16),
        buf((10, 512, 256), F32),
        buf((8, HEAD, 128), F32),
        buf((4, HEAD, 256), F32),
        buf((2048, 128), F32),
        buf((4, N_SEQ // 2, 256, 128), BF16),
        buf((4, N_SEQ * 64, 128), F32),
        pltpu.SemaphoreType.DMA((3,)),
        pltpu.SemaphoreType.DMA((14,)),
        pltpu.SemaphoreType.DMA((14,)),
        pltpu.SemaphoreType.DMA((HEADS,)),
    ]
    sums, w_grad = pl.pallas_call(
        kernel,
        out_shape=(
            jax.ShapeDtypeStruct((256, 128), F32),
            jax.ShapeDtypeStruct((16, WIDTH), F32),
        ),
        in_specs=[vmem, smem, vmem, anywhere, anywhere, anywhere],
        out_specs=(vmem, vmem),
        scratch_shapes=scratch,
        compiler_params=pltpu.CompilerParams(
            collective_id=0, has_side_effects=True, vmem_limit_bytes=48 * 1024 * 1024
        ),
    )(item_rows, lengths, cotangent[0], table, w_in, w_out)
    table_grad = sums.reshape(256, 4, 32).transpose(1, 0, 2).reshape(ROWS_T, 32)
    return table_grad, w_grad


def solution(mesh):
    return jax.shard_map(
        on_device,
        mesh=mesh,
        in_specs=(
            P("table", None),
            P("table", "seq"),
            P("table"),
            P(),
            P(),
            P("table", "seq", None),
        ),
        out_specs=(P("table", "seq"), P("table", None)),
        check_vma=False,
    )
```

time: 514 us -> 106 us (0.21)
  waiting for transfers between devices: 319 us -> 0 us
  Pallas kernels: 0 us -> 97.6 us
  blocking collectives: 70.2 us -> 0 us
  matrix products: 46.3 us -> 0 us
  local copies, waits for them, and re-layouts: 32.1 us -> 6.78 us
  starting transfers between devices: 14.4 us -> 0 us
  other arithmetic: 14.3 us -> 0 us
  between operations: 15.2 us -> 1.31 us
    reduce_scatter x1 -> x0, waiting for transfers between devices: 164 us -> none  [on_device(): lax.psum_scatter(weight_term.astype(jnp.bfloat16), 'table', scatter_dimen...]
    all_gather x4 -> x0, waiting for transfers between devices: 119 us -> none  [the longest x1 39 us: on_device(): key_piece = lax.all_gather(key_loc, 'seq', axis=0, tiled=True)]
    pallas_call x0 -> x1, Pallas kernels: none -> 97.6 us  [on_device(): pl.pallas_call(kernel, out_shape=(jax.ShapeDtypeStruct((256, 128), F32),...]
    psum x1 -> x0, blocking collectives: 48.1 us -> none  [on_device(): w_out_grad = lax.psum(weight_part, 'seq').astype(jnp.float32)]
    dot_general x10 -> x0, matrix products: 46.3 us -> none  [the longest x1 10.5 us: on_device(): jnp.einsum('hqk,khd->qhd', grad_score, key_split, preferred_element_type=...]
    all_to_all x1 -> x0, blocking collectives: 22.1 us -> none  [on_device(): lax.all_to_all(requested, 'table', split_axis=0, concat_axis=0, tiled=True)]
    all_to_all x2 -> x0, waiting for transfers between devices: 20.2 us -> none  [the longest x1 10.3 us: on_device(): lax.all_to_all(outgoing.astype(jnp.bfloat16), 'table', split_axis=0, conc...]
    unnamed x7 -> x0, waiting for transfers between devices: 16 us -> none
  transfers between devices with their start and end apart: 8 -> 0, of which waited for: 8 -> 0; matrix products, arithmetic and copies ran while one was open for 16% -> 0% of each run, Pallas kernels for 0% -> 0%
where the time goes in v1:
time: 106 us
  Pallas kernels  97.6 us (92%)
  local copies, waits for them, and re-layouts  6.78 us (6%)
  between operations  1.31 us (1%)
    pallas_call x1, Pallas kernels, on_device(): pl.pallas_call(kernel, out_shape=(jax.ShapeDtypeStruct((256, 128), F32),...  97.6 us
    unnamed x11, local copies, waits for them, and re-layouts  6.02 us

profile of v1, /device:TPU:1, one launch (start us, length us, event | category | flops | bytes accessed | tf_op | source)
XLA Modules:
  0.0 105.7 jit_solution(2415013301878964423)
XLA Ops:
  1.3 0.0 copy-start
  1.3 1.6 %copy-done = bf16[512,2048]{1,0:T(8,128)(2,1)S(1)} copy-done((bf16[512,2048]{1,0:T(8,128)(2,1)S(1)}, bf16[512,2048]{1,0:T(8,128)(2,1)}, u32[]{:S(2)}) %copy-start) | copy-done | bytes 2097176
  2.9 0.0 copy-start.1
  2.9 1.2 %copy-done.1 = bf16[1024,512]{1,0:T(8,128)(2,1)S(1)} copy-done((bf16[1024,512]{1,0:T(8,128)(2,1)S(1)}, bf16[1024,512]{1,0:T(8,128)(2,1)}, u32[]{:S(2)}) %copy-start.1) | copy-done | bytes 1048600
  4.1 0.0 copy-start.2
  4.1 1.0 copy-done.2
  5.1 0.0 copy-start.3
  5.1 0.9 copy-done.3
  6.0 0.0 copy-start.4
  6.0 0.7 copy-done.4
  6.7 97.6 %shard_map.77 = (f32[256,128]{1,0:T(8,128)S(1)}, f32[16,512]{1,0:T(8,128)S(1)}) custom-call(s32[1,128]{1,0:T(1,128)S(1)} %copy-done.4, s32[1]{0:T(128)S(6)} %copy.14.len_ref, bf16[128,512]{1,0:T(8,128)(2,1)S(1)} %bitcast.6, bf16[1024,512]{1,0:T(8,128)(2,1)S(1)} %copy-done.1, bf16[512,2048]{1,0:T(8,128)(2,1)S(1)} %copy-done, bf16[512,512]{1,0:T(8,128)(2,1)S(1)} %copy-done.2), custom_call_target="tpu_custom_call" | custom-call | tf_op jit(solution)/shard_map/pallas_call | solution.py:594
  104.3 0.1 copy.10
  104.4 0.7 copy.12
  105.1 0.6 copy.15
Async XLA Ops:
  1.3 1.6 %copy-start = (bf16[512,2048]{1,0:T(8,128)(2,1)S(1)}, bf16[512,2048]{1,0:T(8,128)(2,1)}, u32[]{:S(2)}) copy-start(bf16[512,2048]{1,0:T(8,128)(2,1)} %w_in_hbm.1) | copy-start | bytes 6291460
  2.9 1.2 %copy-start.1 = (bf16[1024,512]{1,0:T(8,128)(2,1)S(1)}, bf16[1024,512]{1,0:T(8,128)(2,1)}, u32[]{:S(2)}) copy-start(bf16[1024,512]{1,0:T(8,128)(2,1)} %table_hbm.1) | copy-start | bytes 3145732
  4.1 1.0 copy-start.2
  5.1 0.9 copy-start.3
  6.0 0.7 copy-start.4

commit v2 on v1

--- a/solution.py
+++ b/solution.py
@@ -48,9 +48,9 @@
 
 
 def kernel(
-    rows_ref,
+    rows_hbm,
     len_ref,
-    cot_ref,
+    cot_hbm,
     table_hbm,
     w_in_hbm,
     w_out_hbm,
@@ -59,14 +59,17 @@
     table_v,
     w_in_v,
     w_out_v,
-    ids_send,
+    cot_v,
+    rows_v,
     ids_land,
     fetch_send,
     fetch_land,
     slot_send,
     slot_land,
-    qkv_send,
-    qkv_land,
+    kv_send,
+    kv_own,
+    q_send,
+    q_land,
     kv_sib,
     e_send,
     e_land,
@@ -80,8 +83,10 @@
     part_land,
     sib_send,
     sib_land,
-    back_send,
-    back_land,
+    dkv_send,
+    dkv_land,
+    dq_send,
+    dq_land,
     dx_send,
     dx_land,
     col_send,
@@ -105,7 +110,8 @@
     load_sem,
     send_sem,
     recv_sem,
-    qkv_sem,
+    kv_sem,
+    sib_sem,
 ):
     me_s = lax.axis_index("seq")
     me_t = lax.axis_index("table")
@@ -116,7 +122,13 @@
     loads = [
         pltpu.make_async_copy(src, dst, load_sem.at[k])
         for k, (src, dst) in enumerate(
-            ((table_hbm, table_v), (w_out_hbm, w_out_v), (w_in_hbm, w_in_v))
+            (
+                (rows_hbm, rows_v),
+                (table_hbm, table_v),
+                (cot_hbm, cot_v),
+                (w_out_hbm, w_out_v),
+                (w_in_hbm, w_in_v),
+            )
         )
     ]
     for load in loads:
@@ -149,6 +161,9 @@
             device_id_type=MESH,
         )
 
+    def far_first(n):
+        return 4 + ((n + 1) // 2) * (2 * (n % 2) - 1)
+
     def to_table(src, dst, k, split):
         def body(d, carry):
             peer = (me_t + d) % N_TABLE
@@ -159,22 +174,22 @@
 
     def to_seq(src, dst, k, split):
         def body(d, carry):
-            peer = (me_s + d) % N_SEQ
+            peer = 2 * ((y + far_first(d // 2)) % HEADS) + (core + 1 + d) % 2
             remote(src.at[peer] if split else src, dst.at[me_s], k, {"seq": peer}).start()
             return carry
 
-        lax.fori_loop(1, N_SEQ, body, 0)
+        lax.fori_loop(0, N_SEQ - 1, body, 0)
 
     def to_heads(src, dst, k, split, sems=None):
         def body(d, carry):
-            peer = (y + d) % HEADS
+            peer = (y + far_first(d)) % HEADS
             recv = None if sems is None else sems.at[y]
             remote(
                 src.at[peer] if split else src, dst.at[y], k, {"seq": 2 * peer + core}, recv
             ).start()
             return carry
 
-        lax.fori_loop(1, HEADS, body, 0)
+        lax.fori_loop(0, HEADS - 1, body, 0)
 
     def wait_recv(ref, k):
         pltpu.make_async_copy(ref, ref, recv_sem.at[k]).wait()
@@ -182,12 +197,11 @@
     def wait_sent(ref, k):
         pltpu.make_async_copy(ref, ref, send_sem.at[k]).wait()
 
-    ids_row = rows_ref[...]
-    ids_own = jnp.broadcast_to(ids_row, (8, EVENTS))
-    ids_send[...] = ids_own
-    ids_land[me_t] = ids_own
+    loads[0].wait()
+    ids_row = rows_v[...]
+    ids_land[me_t] = ids_row
     pl.semaphore_wait(barrier, N_TABLE - 1 + N_SEQ - 1)
-    to_table(ids_send, ids_land, 0, False)
+    to_table(rows_v, ids_land, 0, False)
 
     square = (EVENTS, EVENTS)
     row_of, col_of = iota(square, 0), iota(square, 1)
@@ -210,21 +224,22 @@
     half = iota((EVENTS, 1), 0)
     span = jnp.where(half < 64, me_s, 2 * N_SEQ - 1 - me_s)
     live = (span * 64 + (half & 63)) < len_ref[0]
-    grad = jnp.where(live, cot_ref[...].astype(F32), 0.0)
+    loads[2].wait()
+    grad = jnp.where(live, cot_v[...].astype(F32), 0.0)
     grad_b = grad.astype(BF16)
     grad_s[...] = grad
-    loads[1].wait()
+    loads[3].wait()
     dz_t[...] = mm_t(w_out_v[...], grad_b)
 
     wait_recv(ids_land.at[pl.ds(0, N_TABLE - 1)], 0)
-    ids = ids_land[...].reshape(SLOTS, EVENTS)
+    ids = jnp.broadcast_to(ids_land[...], (N_TABLE, CAP, EVENTS)).reshape(SLOTS, EVENTS)
     mine = (ids >> 10) == me_t
     before = one_hot(row_of < col_of)
     rank = mm(one_hot(mine), before)
     turn = (iota((SLOTS, EVENTS), 0) & 7).astype(F32)
     picked = jnp.where(mine & (rank == turn), (ids & 1023).astype(F32) + 1.0, 0.0)
     asked = jnp.sum(picked, axis=1, keepdims=True) - 1.0
-    loads[0].wait()
+    loads[1].wait()
     hot = one_hot(iota((SLOTS, ROWS_T), 1) == asked.astype(I32))
 
     def stack_halves(values):
@@ -248,7 +263,7 @@
     place = iota((EVENTS, 2 * SLOTS), 1)
     pick_lo = one_hot(place == slot_col)
     pick_hi = one_hot(place == slot_col + CAP)
-    loads[2].wait()
+    loads[4].wait()
     wait_recv(fetch_land.at[pl.ds(0, N_TABLE - 1)], 1)
     fetched = fetch_land[...].reshape(2 * SLOTS, 256)
     emb = jnp.concatenate([mm(pick_lo, fetched), mm(pick_hi, fetched)], axis=1)
@@ -266,20 +281,24 @@
         slope_s[:, cols] = sigma * (1.0 + pre * (1.0 - sigma))
         return (pre * sigma).astype(BF16).astype(F32)
 
-    values, queries, keys = project(1), project(2) * 0.0625, project(3)
     lane_e = left((EVENTS, 128))
     lane_h = left((HEAD, 128))
+    keys, values = project(3), project(1)
     for p in range(4):
         cols = slice(128 * p, 128 * p + 128)
-        kt, vt, qt = keys[:, cols], values[:, cols], queries[:, cols]
-        q_lo, q_hi = qt[:64], qt[64:]
-        qkv_send[2 * p, 0:128] = jnp.where(lane_e, kt, swap(vt)).astype(BF16)
-        qkv_send[2 * p + 1, 0:128] = jnp.where(lane_e, swap(kt), vt).astype(BF16)
-        qkv_send[2 * p, 128:192] = jnp.where(lane_h, q_lo, swap(q_hi)).astype(BF16)
-        qkv_send[2 * p + 1, 128:192] = jnp.where(lane_h, swap(q_lo), q_hi).astype(BF16)
-    to_heads(qkv_send, qkv_land, 3, True, qkv_sem)
-    qkv_land[y] = qkv_send[y]
-
+        kt, vt = keys[:, cols], values[:, cols]
+        kv_send[2 * p] = jnp.where(lane_e, kt, swap(vt)).astype(BF16)
+        kv_send[2 * p + 1] = jnp.where(lane_e, swap(kt), vt).astype(BF16)
+    to_heads(kv_send, kv_own, 3, True, kv_sem)
+    kv_own[y] = kv_send[y]
+    queries = project(2) * 0.0625
+    for p in range(4):
+        cols = slice(128 * p, 128 * p + 128)
+        q_lo, q_hi = queries[:64, cols], queries[64:, cols]
+        q_send[2 * p] = jnp.where(lane_h, q_lo, swap(q_hi)).astype(BF16)
+        q_send[2 * p + 1] = jnp.where(lane_h, swap(q_lo), q_hi).astype(BF16)
+    to_heads(q_send, q_land, 14, True)
+    q_land[y] = q_send[y]
     gate = project(0)
     gate_t = gate.T
     u_t[...] = gate_t
@@ -289,25 +308,42 @@
     to_heads(e_send, e_land, 4, True)
     e_land[y] = e_send[y]
 
+    wait_recv(slot_land.at[pl.ds(0, N_SEQ - 1)], 2)
+    lane_8 = left((8, 128))
+
+    def prepare(pair, carry):
+        both = jnp.where(lane_8, slot_land[2 * pair], slot_land[2 * pair + 1]).astype(I32)
+        span_rows = pl.ds(pl.multiple_of(128 * pair, 128), 128)
+        for q in range(4):
+            line = both[q : q + 1]
+            hot_hi[q, pair] = one_hot(iota((256, 128), 0) == (line & 255))
+            column = jnp.broadcast_to((line >> 8).astype(F32), square).T
+            mask_lo[q, span_rows] = jnp.where(
+                (col_of >> 5).astype(F32) == column, 1.0, 0.0
+            )
+        return carry
+
+    lax.fori_loop(0, N_SEQ // 2, prepare, 0)
+
     def pass_on(d, carry):
-        peer = (y + HEADS - d) % HEADS
+        peer = (y + far_first(7 - d)) % HEADS
 
         @pl.when(d > 0)
         def _():
-            pltpu.make_async_copy(qkv_land.at[peer], qkv_land.at[peer], qkv_sem.at[peer]).wait()
-
-        remote(
-            qkv_land.at[peer, pl.ds(0, 128)], kv_sib.at[peer], 5, {"seq": sibling}
-        ).start()
+            pltpu.make_async_copy(kv_own.at[peer], kv_own.at[peer], kv_sem.at[peer]).wait()
+
+        remote(kv_own.at[peer], kv_sib.at[peer], 5, {"seq": sibling}).start()
         return carry
 
     lax.fori_loop(0, HEADS, pass_on, 0)
 
     for i in range(HEADS):
-        block = qkv_land[i]
+        block = kv_own[i]
         kv_nat[pl.ds(pl.multiple_of((2 * i + core) * 64, 64), 64)] = block[0:64]
         kv_nat[pl.ds(pl.multiple_of((31 - 2 * i - core) * 64, 64), 64)] = block[64:128]
-        packed = block[128:192].astype(F32)
+    wait_recv(q_land.at[pl.ds(0, HEADS - 1)], 14)
+    for i in range(HEADS):
+        packed = q_land[i].astype(F32)
         q_pad[64 * i : 64 * i + 64] = jnp.where(lane_h, packed, 0.0).astype(BF16)
         q_pad[64 * (15 - i) : 64 * (16 - i)] = jnp.where(lane_h, swap(packed), 0.0).astype(BF16)
     wait_recv(kv_sib, 5)
@@ -334,7 +370,7 @@
             th = jnp.tanh(h)
             a = (h + h * th).astype(BF16)
             a_t[index] = a
-            g_t[index] = (1.0 + th) + h * (1.0 - th * th)
+            g_t[index] = h
             return total + mm(kv_t[k, 64:128], a)
 
         total = lax.fori_loop(0, t + 1, inner, jnp.zeros((HEAD, 256), F32))
@@ -364,22 +400,13 @@
     stat_land[y] = stats
     to_heads(stat_send, stat_land, 6, False)
 
-    wait_recv(slot_land.at[pl.ds(0, N_SEQ - 1)], 2)
-    lane_8 = left((8, 128))
-
-    def prepare(pair, carry):
-        both = jnp.where(lane_8, slot_land[2 * pair], slot_land[2 * pair + 1]).astype(I32)
-        span_rows = pl.ds(pl.multiple_of(128 * pair, 128), 128)
-        for q in range(4):
-            line = both[q : q + 1]
-            hot_hi[q, pair] = one_hot(iota((256, 128), 0) == (line & 255))
-            column = jnp.broadcast_to((line >> 8).astype(F32), square).T
-            mask_lo[q, span_rows] = jnp.where(
-                (col_of >> 5).astype(F32) == column, 1.0, 0.0
-            )
+    def slopes(index, carry):
+        h = g_t[index]
+        th = jnp.tanh(h)
+        g_t[index] = (1.0 + th) + h * (1.0 - th * th)
         return carry
 
-    lax.fori_loop(0, N_SEQ // 2, prepare, 0)
+    lax.fori_loop(0, 10, slopes, 0)
 
     wait_recv(stat_land.at[pl.ds(0, HEADS - 1)], 6)
     st = stat_land[...]
@@ -422,8 +449,6 @@
         dkv_s[pl.ds(pl.multiple_of(512 * k, 512), 512)] = total
         return carry
 
-    lax.fori_loop(0, 4, backward, 0)
-
     def both_halves(first, second):
         return jnp.concatenate(
             [
@@ -433,23 +458,47 @@
             axis=0,
         )
 
-    for i in range(HEADS):
-        sib_send[i] = both_halves(2 * i + 1 - core, 30 - 2 * i + core).astype(BF16)
-    sibling_copy = remote(sib_send, sib_land, 8, {"seq": sibling})
-    sibling_copy.start()
-
+    def to_sibling(part):
+        for i in range(4 * part, 4 * part + 4):
+            sib_send[i] = both_halves(2 * i + 1 - core, 30 - 2 * i + core).astype(BF16)
+        span = pl.ds(4 * part, 4)
+        remote(sib_send.at[span], sib_land.at[span], 8, {"seq": sibling}, sib_sem.at[part]).start()
+
+    def to_sources(part):
+        span = pl.ds(4 * part, 4)
+        pltpu.make_async_copy(sib_land.at[span], sib_land.at[span], sib_sem.at[part]).wait()
+        for i in range(4 * part, 4 * part + 4):
+            own = both_halves(2 * i + core, 31 - 2 * i - core) + sib_land[i].astype(F32)
+            dkv_send[i] = own.astype(BF16)
+
+        def body(d, carry):
+            peer = (y + far_first(d)) % HEADS
+
+            @pl.when(peer // 4 == part)
+            def _():
+                remote(dkv_send.at[peer], dkv_land.at[y], 9, {"seq": 2 * peer + core}).start()
+
+            return carry
+
+        lax.fori_loop(0, HEADS - 1, body, 0)
+
+    backward(1, 0)
+    backward(2, 0)
+    to_sibling(1)
+    backward(3, 0)
+    to_sources(1)
+    backward(0, 0)
+    to_sibling(0)
     dq_tiles = []
     for t in range(4):
         both = dq_t[t] * 0.0625
         dq_tiles += [both[:, :128], both[:, 128:]]
     for i in range(HEADS):
-        back_send[i, 128:192] = by_source(dq_tiles, i).astype(BF16)
-    wait_recv(sib_land, 8)
-    for i in range(HEADS):
-        own = both_halves(2 * i + core, 31 - 2 * i - core) + sib_land[i].astype(F32)
-        back_send[i, 0:128] = own.astype(BF16)
-    to_heads(back_send, back_land, 9, True)
-    back_land[y] = back_send[y]
+        dq_send[i] = by_source(dq_tiles, i).astype(BF16)
+    to_heads(dq_send, dq_land, 13, True)
+    dq_land[y] = dq_send[y]
+    to_sources(0)
+    dkv_land[y] = dkv_send[y]
 
     wait_recv(ny_land.at[pl.ds(0, HEADS - 1)], 7)
     ny_full = ny_land[...].reshape(WIDTH, EVENTS).astype(F32)
@@ -459,14 +508,15 @@
     w_land[me_t] = w_send[me_t]
     d_u = (dz_t[...] * ny_full).T
 
-    wait_recv(back_land.at[pl.ds(0, HEADS - 1)], 9)
+    wait_recv(dkv_land.at[pl.ds(0, HEADS - 1)], 9)
+    wait_recv(dq_land.at[pl.ds(0, HEADS - 1)], 13)
     d_k, d_v, d_q = [], [], []
     for p in range(4):
-        first = back_land[2 * p, 0:128].astype(F32)
-        second = back_land[2 * p + 1, 0:128].astype(F32)
+        first = dkv_land[2 * p].astype(F32)
+        second = dkv_land[2 * p + 1].astype(F32)
         d_k.append(jnp.where(lane_e, first, swap(second)))
         d_v.append(jnp.where(lane_e, swap(first), second))
-        pair = [back_land[2 * p + n, 128:192].astype(F32) for n in range(2)]
+        pair = [dq_land[2 * p + n].astype(F32) for n in range(2)]
         d_q.append(jnp.concatenate(pair, axis=0).T)
     d_proj = jnp.concatenate([d_u] + d_v + d_q + d_k, axis=1)
     d_pre = (d_proj * slope_s[...]).astype(BF16)
@@ -499,7 +549,7 @@
                 for q in range(1, 4):
                     chunk = jnp.where(group == q, turned[(q - g) % 4][64 * q : 64 * q + 64], chunk)
                 col_send[8 * side + 4 * tile + g] = chunk.astype(BF16)
-    to_seq(col_send, col_land, 13, True)
+    to_seq(col_send, col_land, 15, True)
     col_land[me_s] = col_send[me_s]
 
     wait_recv(part_land.at[pl.ds(0, N_SEQ - 1)], 12)
@@ -509,29 +559,33 @@
     spread_to = one_hot(
         iota((128, WIDTH), 0) == 32 * (spread_of >> 7) + (spread_of & 31)
     )
-    wait_recv(col_land.at[pl.ds(0, N_SEQ - 1)], 13)
+    wait_recv(col_land.at[pl.ds(0, N_SEQ - 1)], 15)
     wide = mm(col_land[...].reshape(N_SEQ * 64, 128), spread_to)
     total = jnp.zeros((256, 128), F32)
     for q in range(4):
         placed = (wide[:, 128 * q : 128 * q + 128] * mask_lo[q]).astype(BF16)
         hot_q = jnp.concatenate([hot_hi[q, pair] for pair in range(N_SEQ // 2)], axis=1)
         total = total + mm(hot_q, placed)
-    out_ref[...] = total
+    turned = total.T
+    for k in range(4):
+        out_ref[:, 256 * k : 256 * k + 256] = turned[32 * k : 32 * k + 32]
 
     wait_sent(ids_land.at[pl.ds(0, N_TABLE - 1)], 0)
     wait_sent(fetch_send.at[pl.ds(0, N_TABLE - 1)], 1)
     wait_sent(slot_land.at[pl.ds(0, N_SEQ - 1)], 2)
-    wait_sent(qkv_send.at[pl.ds(0, HEADS - 1)], 3)
+    wait_sent(kv_send.at[pl.ds(0, HEADS - 1)], 3)
+    wait_sent(q_send.at[pl.ds(0, HEADS - 1)], 14)
     wait_sent(e_send.at[pl.ds(0, HEADS - 1)], 4)
     wait_sent(kv_sib, 5)
     wait_sent(stat_land.at[pl.ds(0, HEADS - 1)], 6)
     wait_sent(ny_send.at[pl.ds(0, HEADS - 1)], 7)
     wait_sent(sib_send, 8)
-    wait_sent(back_send.at[pl.ds(0, HEADS - 1)], 9)
+    wait_sent(dkv_send.at[pl.ds(0, HEADS - 1)], 9)
+    wait_sent(dq_send.at[pl.ds(0, HEADS - 1)], 13)
     wait_sent(w_send.at[pl.ds(0, N_TABLE - 1)], 10)
     wait_sent(dx_send.at[pl.ds(0, N_TABLE - 1)], 11)
     wait_sent(part_land.at[pl.ds(0, N_SEQ - 1)], 12)
-    wait_sent(col_send.at[pl.ds(0, N_SEQ - 1)], 13)
+    wait_sent(col_send.at[pl.ds(0, N_SEQ - 1)], 15)
 
 
 def on_device(table, item_rows, lengths, w_in, w_out, cotangent):
@@ -543,14 +597,17 @@
         buf((ROWS_T, WIDTH), BF16),
         buf((WIDTH, 4 * WIDTH), BF16),
         buf((WIDTH, WIDTH), BF16),
-        buf((8, EVENTS), I32),
-        buf((N_TABLE, 8, EVENTS), I32),
+        buf((EVENTS, WIDTH), BF16),
+        buf((1, EVENTS), I32),
+        buf((N_TABLE, 1, EVENTS), I32),
         buf((N_TABLE, 16, 256), BF16),
         buf((N_TABLE, 16, 256), BF16),
         buf((8, 128), F32),
         buf((N_SEQ, 8, 128), F32),
-        buf((HEADS, 192, 128), BF16),
-        buf((HEADS, 192, 128), BF16),
+        buf((HEADS, 128, 128), BF16),
+        buf((HEADS, 128, 128), BF16),
+        buf((HEADS, HEAD, 128), BF16),
+        buf((HEADS, HEAD, 128), BF16),
         buf((HEADS, 128, 128), BF16),
         buf((HEADS, HEAD, 128), BF16),
         buf((HEADS, HEAD, 128), BF16),
@@ -564,8 +621,10 @@
         buf((N_SEQ, 16, WIDTH), BF16),
         buf((HEADS, 128, 128), BF16),
         buf((HEADS, 128, 128), BF16),
-        buf((HEADS, 192, 128), BF16),
-        buf((HEADS, 192, 128), BF16),
+        buf((HEADS, 128, 128), BF16),
+        buf((HEADS, 128, 128), BF16),
+        buf((HEADS, HEAD, 128), BF16),
+        buf((HEADS, HEAD, 128), BF16),
         buf((N_TABLE, 16, 256), BF16),
         buf((N_TABLE, 16, 256), BF16),
         buf((N_SEQ, 64, 128), BF16),
@@ -586,26 +645,26 @@
         buf((2048, 128), F32),
         buf((4, N_SEQ // 2, 256, 128), BF16),
         buf((4, N_SEQ * 64, 128), F32),
-        pltpu.SemaphoreType.DMA((3,)),
-        pltpu.SemaphoreType.DMA((14,)),
-        pltpu.SemaphoreType.DMA((14,)),
+        pltpu.SemaphoreType.DMA((5,)),
+        pltpu.SemaphoreType.DMA((16,)),
+        pltpu.SemaphoreType.DMA((16,)),
         pltpu.SemaphoreType.DMA((HEADS,)),
+        pltpu.SemaphoreType.DMA((2,)),
     ]
     sums, w_grad = pl.pallas_call(
         kernel,
         out_shape=(
-            jax.ShapeDtypeStruct((256, 128), F32),
+            jax.ShapeDtypeStruct((32, ROWS_T), F32),
             jax.ShapeDtypeStruct((16, WIDTH), F32),
         ),
-        in_specs=[vmem, smem, vmem, anywhere, anywhere, anywhere],
+        in_specs=[anywhere, smem, anywhere, anywhere, anywhere, anywhere],
         out_specs=(vmem, vmem),
         scratch_shapes=scratch,
         compiler_params=pltpu.CompilerParams(
-            collective_id=0, has_side_effects=True, vmem_limit_bytes=48 * 1024 * 1024
+            collective_id=0, has_side_effects=True, vmem_limit_bytes=60 * 1024 * 1024
         ),
     )(item_rows, lengths, cotangent[0], table, w_in, w_out)
-    table_grad = sums.reshape(256, 4, 32).transpose(1, 0, 2).reshape(ROWS_T, 32)
-    return table_grad, w_grad
+    return sums.T, w_grad
 
 
 def solution(mesh):

time: 106 us -> 95.5 us (0.901)
  Pallas kernels: 97.6 us -> 91.1 us
  local copies, waits for them, and re-layouts: 6.78 us -> 2.94 us
    pallas_call x1, Pallas kernels: 97.6 us -> 91.1 us  [on_device(): pl.pallas_call(kernel, out_shape=(jax.ShapeDtypeStruct((32, ROWS_T), F32)...]
    unnamed x11 -> x2, local copies, waits for them, and re-layouts: 6.02 us -> 2.94 us
where the time goes in v2:
time: 95.5 us; the launch traced here: 95.3 us
  Pallas kernels  91.1 us (95%)
  local copies, waits for them, and re-layouts  2.94 us (3%)
  between operations  1.28 us (1%)
    pallas_call x1, Pallas kernels, on_device(): pl.pallas_call(kernel, out_shape=(jax.ShapeDtypeStruct((32, ROWS_T), F32)...  91.1 us
    unnamed x2, local copies, waits for them, and re-layouts  2.94 us

profile of v2, /device:TPU:1, one launch (start us, length us, event | category | flops | bytes accessed | tf_op | source)
XLA Modules:
  0.0 95.3 jit_solution(4509533435999322993)
XLA Ops:
  1.3 91.1 %shard_map.77 = (f32[32,1024]{1,0:T(8,128)}, f32[16,512]{1,0:T(8,128)}) custom-call(s32[1,128]{1,0:T(1,128)} %rows_hbm.1, s32[1]{0:T(128)S(6)} %copy.10.len_ref, bf16[128,512]{1,0:T(8,128)(2,1)} %bitcast.2, bf16[1024,512]{1,0:T(8,128)(2,1)} %table_hbm.1, bf16[512,2048]{1,0:T(8,128)(2,1)} %w_in_hbm.1, bf16[512,512]{1,0:T(8,128)(2,1)} %w_out_hbm.1), custom_call_target="tpu_custom_call" | custom-call | tf_op jit(solution)/shard_map/pallas_call | solution.py:654
  92.3 1.6 %copy.11 = f32[1024,32]{0,1:T(8,128)} copy(f32[1024,32]{0,1:T(8,128)} %bitcast.3) | data formatting | bytes 262144
  93.9 1.4 %copy.12 = f32[16,512]{1,0:T(8,128)} copy(f32[16,512]{1,0:T(8,128)} %get-tuple-element.9) | data formatting | bytes 65536

commit v3 on v2

--- a/solution.py
+++ b/solution.py
@@ -107,6 +107,7 @@
     dkv_s,
     hot_hi,
     mask_lo,
+    asked_s,
     load_sem,
     send_sem,
     recv_sem,
@@ -172,6 +173,16 @@
 
         lax.fori_loop(1, N_TABLE, body, 0)
 
+    def to_table_group(src, dst, k, group):
+        def body(d, carry):
+            z = (me_t // 4 + far_first(d // 4)) % 8
+            x = (me_t + 2 + ((d % 4 + 1) // 2) * (2 * (d % 2) - 1)) % 4
+            peer = 4 * z + x
+            remote(src.at[peer], dst.at[me_t], k, {"table": peer}).start()
+            return carry
+
+        lax.fori_loop(16 * group, 16 + 15 * group, body, 0)
+
     def to_seq(src, dst, k, split):
         def body(d, carry):
             peer = 2 * ((y + far_first(d // 2)) % HEADS) + (core + 1 + d) % 2
@@ -196,6 +207,9 @@
 
     def wait_sent(ref, k):
         pltpu.make_async_copy(ref, ref, send_sem.at[k]).wait()
+
+    def z_rows(n):
+        return pl.multiple_of(32 * ((me_t // 4 + 6 + n) % 8), 32)
 
     loads[0].wait()
     ids_row = rows_v[...]
@@ -250,12 +264,12 @@
     to_table(fetch_send, fetch_land, 1, True)
     fetch_land[me_t] = fetch_send[me_t]
 
+    asked_s[...] = jnp.broadcast_to(asked, (SLOTS, 128))
     tiles = []
-    for q in range(4):
-        piece = asked[64 * q : 64 * q + 64]
-        twice = jnp.concatenate([piece, piece], axis=0)
-        tiles.append(jnp.broadcast_to(twice, square).T[0:1])
-    slots = jnp.concatenate(tiles + tiles, axis=0)
+    for n in range(8):
+        piece = asked_s[pl.ds(z_rows(n), 32)]
+        tiles.append(jnp.concatenate([piece] * 4, axis=0).T[0:1])
+    slots = jnp.concatenate(tiles, axis=0)
     slot_send[...] = slots
     slot_land[me_s] = slots
     to_seq(slot_send, slot_land, 2, False)
@@ -309,21 +323,22 @@
     e_land[y] = e_send[y]
 
     wait_recv(slot_land.at[pl.ds(0, N_SEQ - 1)], 2)
-    lane_8 = left((8, 128))
-
-    def prepare(pair, carry):
-        both = jnp.where(lane_8, slot_land[2 * pair], slot_land[2 * pair + 1]).astype(I32)
-        span_rows = pl.ds(pl.multiple_of(128 * pair, 128), 128)
-        for q in range(4):
-            line = both[q : q + 1]
-            hot_hi[q, pair] = one_hot(iota((256, 128), 0) == (line & 255))
+    part_8 = iota((8, 128), 1) >> 5
+
+    def prepare(quad, carry):
+        four = slot_land[4 * quad]
+        for n in range(1, 4):
+            four = jnp.where(part_8 == n, slot_land[4 * quad + n], four)
+        four = four.astype(I32)
+        span_rows = pl.ds(pl.multiple_of(128 * quad, 128), 128)
+        for n in range(8):
+            line = four[n : n + 1]
+            hot_hi[n, quad] = one_hot(iota((256, 128), 0) == (line & 255))
             column = jnp.broadcast_to((line >> 8).astype(F32), square).T
-            mask_lo[q, span_rows] = jnp.where(
-                (col_of >> 5).astype(F32) == column, 1.0, 0.0
-            )
+            mask_lo[n, span_rows] = jnp.where((col_of >> 5).astype(F32) == column, 1.0, 0.0)
         return carry
 
-    lax.fori_loop(0, N_SEQ // 2, prepare, 0)
+    lax.fori_loop(0, N_SEQ // 4, prepare, 0)
 
     def pass_on(d, carry):
         peer = (y + far_first(7 - d)) % HEADS
@@ -341,11 +356,6 @@
         block = kv_own[i]
         kv_nat[pl.ds(pl.multiple_of((2 * i + core) * 64, 64), 64)] = block[0:64]
         kv_nat[pl.ds(pl.multiple_of((31 - 2 * i - core) * 64, 64), 64)] = block[64:128]
-    wait_recv(q_land.at[pl.ds(0, HEADS - 1)], 14)
-    for i in range(HEADS):
-        packed = q_land[i].astype(F32)
-        q_pad[64 * i : 64 * i + 64] = jnp.where(lane_h, packed, 0.0).astype(BF16)
-        q_pad[64 * (15 - i) : 64 * (16 - i)] = jnp.where(lane_h, swap(packed), 0.0).astype(BF16)
     wait_recv(kv_sib, 5)
     for i in range(HEADS):
         block = kv_sib[i]
@@ -353,6 +363,11 @@
         kv_nat[pl.ds(pl.multiple_of((30 - 2 * i + core) * 64, 64), 64)] = block[64:128]
     for k in range(4):
         kv_t[k] = kv_nat[512 * k : 512 * k + 512].T
+    wait_recv(q_land.at[pl.ds(0, HEADS - 1)], 14)
+    for i in range(HEADS):
+        packed = q_land[i].astype(F32)
+        q_pad[64 * i : 64 * i + 64] = jnp.where(lane_h, packed, 0.0).astype(BF16)
+        q_pad[64 * (15 - i) : 64 * (16 - i)] = jnp.where(lane_h, swap(packed), 0.0).astype(BF16)
 
     def forward(t, carry):
         q = q_pad[pl.ds(pl.multiple_of(256 * t, 256), 256)]
@@ -434,10 +449,12 @@
 
     dq_t[...] = jnp.zeros_like(dq_t)
 
-    def backward(k, carry):
-        kv = kv_nat[pl.ds(pl.multiple_of(512 * k, 512), 512)]
-
-        def inner(t, total):
+    def backward(k, first, step, count, fresh):
+        span_k = pl.ds(512 * k, 512)
+        kv = kv_nat[span_k]
+
+        def inner(n, total):
+            t = first + step * n
             index = t * (t + 1) // 2 + k
             span_q = pl.ds(pl.multiple_of(256 * t, 256), 256)
             dy_q = dy_pad[span_q]
@@ -445,9 +462,8 @@
             dq_t[t] += mm(kv_t[k, 0:64], ds)
             return total + mm(ds, q_pad[span_q]) + mm(a_t[index], dy_q)
 
-        total = lax.fori_loop(k, 4, inner, jnp.zeros((512, 128), F32))
-        dkv_s[pl.ds(pl.multiple_of(512 * k, 512), 512)] = total
-        return carry
+        start = jnp.zeros((512, 128), F32) if fresh else dkv_s[span_k]
+        dkv_s[span_k] = lax.fori_loop(0, count, inner, start)
 
     def both_halves(first, second):
         return jnp.concatenate(
@@ -471,35 +487,35 @@
             own = both_halves(2 * i + core, 31 - 2 * i - core) + sib_land[i].astype(F32)
             dkv_send[i] = own.astype(BF16)
 
+        some_heads(dkv_send, dkv_land, 9, part)
+
+    def some_heads(src, dst, k, part):
         def body(d, carry):
             peer = (y + far_first(d)) % HEADS
 
             @pl.when(peer // 4 == part)
             def _():
-                remote(dkv_send.at[peer], dkv_land.at[y], 9, {"seq": 2 * peer + core}).start()
+                remote(src.at[peer], dst.at[y], k, {"seq": 2 * peer + core}).start()
 
             return carry
 
         lax.fori_loop(0, HEADS - 1, body, 0)
 
-    backward(1, 0)
-    backward(2, 0)
+    def queries_back(part):
+        dq_tiles = []
+        for t in range(4):
+            if (t in (1, 2)) == (part == 1):
+                both = dq_t[t] * 0.0625
+                dq_tiles += [both[:, :128], both[:, 128:]]
+            else:
+                dq_tiles += [None, None]
+        for i in range(4 * part, 4 * part + 4):
+            dq_send[i] = by_source(dq_tiles, i).astype(BF16)
+        some_heads(dq_send, dq_land, 13, part)
+
+    backward(1, 1, 1, 3, True)
+    backward(2, 2, 1, 2, True)
     to_sibling(1)
-    backward(3, 0)
-    to_sources(1)
-    backward(0, 0)
-    to_sibling(0)
-    dq_tiles = []
-    for t in range(4):
-        both = dq_t[t] * 0.0625
-        dq_tiles += [both[:, :128], both[:, 128:]]
-    for i in range(HEADS):
-        dq_send[i] = by_source(dq_tiles, i).astype(BF16)
-    to_heads(dq_send, dq_land, 13, True)
-    dq_land[y] = dq_send[y]
-    to_sources(0)
-    dkv_land[y] = dkv_send[y]
-
     wait_recv(ny_land.at[pl.ds(0, HEADS - 1)], 7)
     ny_full = ny_land[...].reshape(WIDTH, EVENTS).astype(F32)
     z_t = (ny_full * u_t[...]).astype(BF16)
@@ -507,6 +523,18 @@
     to_table(w_send, w_land, 10, True)
     w_land[me_t] = w_send[me_t]
     d_u = (dz_t[...] * ny_full).T
+    backward(0, 1, 1, 2, True)
+    queries_back(1)
+    to_sources(1)
+    backward(0, 0, 3, 2, False)
+    backward(3, 3, 1, 1, True)
+    to_sibling(0)
+    queries_back(0)
+    to_sources(0)
+    dq_land[y] = dq_send[y]
+    dkv_land[y] = dkv_send[y]
+    d_pre_u = (d_u * slope_s[:, 0:WIDTH]).astype(BF16)
+    dn_u = mm_t(d_pre_u, w_in_v[:, 0:WIDTH])
 
     wait_recv(dkv_land.at[pl.ds(0, HEADS - 1)], 9)
     wait_recv(dq_land.at[pl.ds(0, HEADS - 1)], 13)
@@ -518,9 +546,9 @@
         d_v.append(jnp.where(lane_e, swap(first), second))
         pair = [dq_land[2 * p + n].astype(F32) for n in range(2)]
         d_q.append(jnp.concatenate(pair, axis=0).T)
-    d_proj = jnp.concatenate([d_u] + d_v + d_q + d_k, axis=1)
-    d_pre = (d_proj * slope_s[...]).astype(BF16)
-    dn = mm_t(d_pre, w_in_v[...])
+    d_proj = jnp.concatenate(d_v + d_q + d_k, axis=1)
+    d_pre = (d_proj * slope_s[:, WIDTH:]).astype(BF16)
+    dn = dn_u + mm_t(d_pre, w_in_v[:, WIDTH:])
     nx = nx_s[...]
     first = jnp.mean(dn, axis=1, keepdims=True)
     second = jnp.mean(dn * nx, axis=1, keepdims=True)
@@ -528,7 +556,8 @@
 
     place_t = one_hot(iota((SLOTS, EVENTS), 0) == slot_row)
     dx_send[...] = stack_halves(mm(place_t, d_x.astype(BF16)))
-    to_table(dx_send, dx_land, 11, True)
+    to_table_group(dx_send, dx_land, 11, 1)
+    to_table_group(dx_send, dx_land, 16, 0)
     dx_land[me_t] = dx_send[me_t]
 
     wait_recv(w_land.at[pl.ds(0, N_TABLE - 1)], 10)
@@ -537,35 +566,52 @@
     part_land[me_s] = part
     to_seq(part_send, part_land, 12, False)
 
-    wait_recv(dx_land.at[pl.ds(0, N_TABLE - 1)], 11)
-    group = iota((64, 128), 1) >> 5
-    for side in range(2):
-        rows = dx_land[:, 8 * side : 8 * side + 8].astype(F32).reshape(SLOTS, 256)
-        for tile in range(2):
-            cut = rows[:, 128 * tile : 128 * tile + 128]
-            turned = [cut] + [pltpu.roll(cut, 32 * r, 1) for r in range(1, 4)]
-            for g in range(4):
-                chunk = turned[(0 - g) % 4][0:64]
-                for q in range(1, 4):
-                    chunk = jnp.where(group == q, turned[(q - g) % 4][64 * q : 64 * q + 64], chunk)
-                col_send[8 * side + 4 * tile + g] = chunk.astype(BF16)
-    to_seq(col_send, col_land, 15, True)
-    col_land[me_s] = col_send[me_s]
-
-    wait_recv(part_land.at[pl.ds(0, N_SEQ - 1)], 12)
-    w_grad_ref[...] = jnp.sum(part_land[...].astype(F32), axis=0)
-
+    group = iota((32, 128), 1) >> 5
     spread_of = iota((128, WIDTH), 1)
     spread_to = one_hot(
         iota((128, WIDTH), 0) == 32 * (spread_of >> 7) + (spread_of & 31)
     )
-    wait_recv(col_land.at[pl.ds(0, N_SEQ - 1)], 15)
-    wide = mm(col_land[...].reshape(N_SEQ * 64, 128), spread_to)
-    total = jnp.zeros((256, 128), F32)
-    for q in range(4):
-        placed = (wide[:, 128 * q : 128 * q + 128] * mask_lo[q]).astype(BF16)
-        hot_q = jnp.concatenate([hot_hi[q, pair] for pair in range(N_SEQ // 2)], axis=1)
-        total = total + mm(hot_q, placed)
+
+    def columns(side):
+        planes = [
+            dx_land[pl.ds(pl.multiple_of(4 * ((me_t // 4 + 6 + n) % 8), 4), 4)].astype(F32)
+            for n in range(4 * side, 4 * side + 4)
+        ]
+        for part in range(2):
+            rows = [plane[:, 8 * part : 8 * part + 8].reshape(32, 256) for plane in planes]
+            for tile in range(2):
+                cuts = [row[:, 128 * tile : 128 * tile + 128] for row in rows]
+                for g in range(4):
+                    chunk = None
+                    for q in range(4):
+                        shift = 32 * ((q - g) % 4)
+                        cut = pltpu.roll(cuts[q], shift, 1) if shift else cuts[q]
+                        chunk = cut if q == 0 else jnp.where(group == q, cut, chunk)
+                    col_send[side, 8 * part + 4 * tile + g] = chunk.astype(BF16)
+        to_seq(col_send.at[side], col_land.at[side], 15 if side == 0 else 17, True)
+        col_land[side, me_s] = col_send[side, me_s]
+
+    def placed(side, total):
+        wide = mm(col_land[side].reshape(N_SEQ * 32, 128), spread_to)
+        for q in range(4):
+            n = 4 * side + q
+            put = (wide[:, 128 * q : 128 * q + 128] * mask_lo[n]).astype(BF16)
+            hot_q = jnp.concatenate([hot_hi[n, quad] for quad in range(N_SEQ // 4)], axis=1)
+            total = total + mm(hot_q, put)
+        return total
+
+    wait_recv(dx_land.at[pl.ds(0, 15)], 11)
+    columns(0)
+    wait_recv(dx_land.at[pl.ds(0, 16)], 16)
+    columns(1)
+
+    wait_recv(part_land.at[pl.ds(0, N_SEQ - 1)], 12)
+    w_grad_ref[...] = jnp.sum(part_land[...].astype(F32), axis=0)
+
+    wait_recv(col_land.at[0, pl.ds(0, N_SEQ - 1)], 15)
+    total = placed(0, jnp.zeros((256, 128), F32))
+    wait_recv(col_land.at[1, pl.ds(0, N_SEQ - 1)], 17)
+    total = placed(1, total)
     turned = total.T
     for k in range(4):
         out_ref[:, 256 * k : 256 * k + 256] = turned[32 * k : 32 * k + 32]
@@ -583,9 +629,11 @@
     wait_sent(dkv_send.at[pl.ds(0, HEADS - 1)], 9)
     wait_sent(dq_send.at[pl.ds(0, HEADS - 1)], 13)
     wait_sent(w_send.at[pl.ds(0, N_TABLE - 1)], 10)
-    wait_sent(dx_send.at[pl.ds(0, N_TABLE - 1)], 11)
+    wait_sent(dx_send.at[pl.ds(0, 15)], 11)
+    wait_sent(dx_send.at[pl.ds(0, 16)], 16)
     wait_sent(part_land.at[pl.ds(0, N_SEQ - 1)], 12)
-    wait_sent(col_send.at[pl.ds(0, N_SEQ - 1)], 15)
+    wait_sent(col_send.at[0, pl.ds(0, N_SEQ - 1)], 15)
+    wait_sent(col_send.at[1, pl.ds(0, N_SEQ - 1)], 17)
 
 
 def on_device(table, item_rows, lengths, w_in, w_out, cotangent):
@@ -627,8 +675,8 @@
         buf((HEADS, HEAD, 128), BF16),
         buf((N_TABLE, 16, 256), BF16),
         buf((N_TABLE, 16, 256), BF16),
-        buf((N_SEQ, 64, 128), BF16),
-        buf((N_SEQ, 64, 128), BF16),
+        buf((2, N_SEQ, 32, 128), BF16),
+        buf((2, N_SEQ, 32, 128), BF16),
         buf((EVENTS, WIDTH), F32),
         buf((WIDTH, EVENTS), F32),
         buf((WIDTH, EVENTS), F32),
@@ -643,25 +691,26 @@
         buf((8, HEAD, 128), F32),
         buf((4, HEAD, 256), F32),
         buf((2048, 128), F32),
-        buf((4, N_SEQ // 2, 256, 128), BF16),
-        buf((4, N_SEQ * 64, 128), F32),
+        buf((8, N_SEQ // 4, 256, 128), BF16),
+        buf((8, N_SEQ * 32, 128), F32),
+        buf((SLOTS, 128), F32),
         pltpu.SemaphoreType.DMA((5,)),
-        pltpu.SemaphoreType.DMA((16,)),
-        pltpu.SemaphoreType.DMA((16,)),
+        pltpu.SemaphoreType.DMA((18,)),
+        pltpu.SemaphoreType.DMA((18,)),
         pltpu.SemaphoreType.DMA((HEADS,)),
         pltpu.SemaphoreType.DMA((2,)),
     ]
     sums, w_grad = pl.pallas_call(
         kernel,
         out_shape=(
-            jax.ShapeDtypeStruct((32, ROWS_T), F32),
-            jax.ShapeDtypeStruct((16, WIDTH), F32),
+            pltpu.VMEM((32, ROWS_T), F32),
+            pltpu.VMEM((16, WIDTH), F32),
         ),
         in_specs=[anywhere, smem, anywhere, anywhere, anywhere, anywhere],
         out_specs=(vmem, vmem),
         scratch_shapes=scratch,
         compiler_params=pltpu.CompilerParams(
-            collective_id=0, has_side_effects=True, vmem_limit_bytes=60 * 1024 * 1024
+            collective_id=0, has_side_effects=True, vmem_limit_bytes=56 * 1024 * 1024
         ),
     )(item_rows, lengths, cotangent[0], table, w_in, w_out)
     return sums.T, w_grad

time: 95.5 us -> 92.3 us (0.966)
  local copies, waits for them, and re-layouts: 2.94 us -> 1.27 us
  Pallas kernels: 91.1 us -> 89.6 us
    unnamed x2, local copies, waits for them, and re-layouts: 2.94 us -> 1.27 us
    pallas_call x1, Pallas kernels: 91.1 us -> 89.6 us  [on_device(): pl.pallas_call(kernel, out_shape=(pltpu.VMEM((32, ROWS_T), F32), pltpu.VM...]
where the time goes in v3:
time: 92.3 us; the launch traced here: 92.1 us
  Pallas kernels  89.6 us (97%)
  between operations  1.28 us (1%)
  local copies, waits for them, and re-layouts  1.27 us (1%)
    pallas_call x1, Pallas kernels, on_device(): pl.pallas_call(kernel, out_shape=(pltpu.VMEM((32, ROWS_T), F32), pltpu.VM...  89.6 us

profile of v3, /device:TPU:1, one launch (start us, length us, event | category | flops | bytes accessed | tf_op | source)
XLA Modules:
  0.0 92.1 jit_solution(1960816097383356254)
XLA Ops:
  1.3 89.6 %shard_map.77 = (f32[32,1024]{1,0:T(8,128)S(1)}, f32[16,512]{1,0:T(8,128)S(1)}) custom-call(s32[1,128]{1,0:T(1,128)} %rows_hbm.1, s32[1]{0:T(128)S(6)} %copy.12.len_ref, bf16[128,512]{1,0:T(8,128)(2,1)} %bitcast.3, bf16[1024,512]{1,0:T(8,128)(2,1)} %table_hbm.1, bf16[512,2048]{1,0:T(8,128)(2,1)} %w_in_hbm.1, bf16[512,512]{1,0:T(8,128)(2,1)} %w_out_hbm.1), custom_call_target="tpu_custom_call" | custom-call | tf_op jit(solution)/shard_map/pallas_call | solution.py:703
  90.9 0.7 copy.10
  91.5 0.6 copy.11

commit v4 on v3

--- a/solution.py
+++ b/solution.py
@@ -77,6 +77,9 @@
     stat_land,
     ny_send,
     ny_land,
+    w_term,
+    w_sib_send,
+    w_sib_land,
     w_send,
     w_land,
     part_send,
@@ -119,6 +122,7 @@
     y = me_s // 2
     core = me_s % 2
     sibling = me_s + 1 - 2 * core
+    owns_w = core == me_t // 16
 
     loads = [
         pltpu.make_async_copy(src, dst, load_sem.at[k])
@@ -341,7 +345,7 @@
     lax.fori_loop(0, N_SEQ // 4, prepare, 0)
 
     def pass_on(d, carry):
-        peer = (y + far_first(7 - d)) % HEADS
+        peer = (y + jnp.where(d == 0, 0, far_first(d - 1))) % HEADS
 
         @pl.when(d > 0)
         def _():
@@ -516,13 +520,6 @@
     backward(1, 1, 1, 3, True)
     backward(2, 2, 1, 2, True)
     to_sibling(1)
-    wait_recv(ny_land.at[pl.ds(0, HEADS - 1)], 7)
-    ny_full = ny_land[...].reshape(WIDTH, EVENTS).astype(F32)
-    z_t = (ny_full * u_t[...]).astype(BF16)
-    w_send[...] = mm(z_t, grad_s[...].astype(BF16)).reshape(N_TABLE, 16, WIDTH).astype(BF16)
-    to_table(w_send, w_land, 10, True)
-    w_land[me_t] = w_send[me_t]
-    d_u = (dz_t[...] * ny_full).T
     backward(0, 1, 1, 2, True)
     queries_back(1)
     to_sources(1)
@@ -531,10 +528,36 @@
     to_sibling(0)
     queries_back(0)
     to_sources(0)
+    wait_recv(ny_land.at[pl.ds(0, HEADS - 1)], 7)
+    ny_full = ny_land[...].reshape(WIDTH, EVENTS).astype(F32)
+    z_t = (ny_full * u_t[...]).astype(BF16)
+    w_term[...] = mm(z_t, grad_s[...].astype(BF16)).reshape(N_TABLE, 16, WIDTH)
+    w_sib_send[...] = w_term[pl.ds(pl.multiple_of(16 - 16 * core, 16), 16)].astype(BF16)
+    remote(w_sib_send, w_sib_land, 18, {"seq": sibling}).start()
+    d_u = (dz_t[...] * ny_full).T
     dq_land[y] = dq_send[y]
     dkv_land[y] = dkv_send[y]
     d_pre_u = (d_u * slope_s[:, 0:WIDTH]).astype(BF16)
     dn_u = mm_t(d_pre_u, w_in_v[:, 0:WIDTH])
+    wait_recv(w_sib_land, 18)
+    w_pair = w_term[pl.ds(pl.multiple_of(16 * core, 16), 16)] + w_sib_land[...].astype(F32)
+    w_send[...] = w_pair.astype(BF16)
+
+    def w_out_to_owner(n, carry):
+        slot = (n + 8 + 4 * (me_t // 4 - 4 * core)) % 16
+        peer = 16 * core + slot
+
+        @pl.when(peer != me_t)
+        def _():
+            remote(w_send.at[slot], w_land.at[me_t], 10, {"table": peer}).start()
+
+        return carry
+
+    lax.fori_loop(0, 16, w_out_to_owner, 0)
+
+    @pl.when(owns_w)
+    def _():
+        w_land[me_t] = w_send[me_t % 16]
 
     wait_recv(dkv_land.at[pl.ds(0, HEADS - 1)], 9)
     wait_recv(dq_land.at[pl.ds(0, HEADS - 1)], 13)
@@ -560,11 +583,19 @@
     to_table_group(dx_send, dx_land, 16, 0)
     dx_land[me_t] = dx_send[me_t]
 
-    wait_recv(w_land.at[pl.ds(0, N_TABLE - 1)], 10)
-    part = jnp.sum(w_land[...].astype(F32), axis=0).astype(BF16)
-    part_send[...] = part
-    part_land[me_s] = part
-    to_seq(part_send, part_land, 12, False)
+    @pl.when(owns_w)
+    def _():
+        wait_recv(w_land.at[pl.ds(0, N_TABLE - 1)], 10)
+        part = jnp.sum(w_land[...].astype(F32), axis=0).astype(BF16)
+        part_send[...] = part
+        part_land[y] = part
+
+        def body(d, carry):
+            peer = 2 * ((y + far_first(d // 2)) % HEADS) + (core + 1 + d) % 2
+            remote(part_send, part_land.at[y], 12, {"seq": peer}).start()
+            return carry
+
+        lax.fori_loop(0, N_SEQ - 1, body, 0)
 
     group = iota((32, 128), 1) >> 5
     spread_of = iota((128, WIDTH), 1)
@@ -605,7 +636,14 @@
     wait_recv(dx_land.at[pl.ds(0, 16)], 16)
     columns(1)
 
-    wait_recv(part_land.at[pl.ds(0, N_SEQ - 1)], 12)
+    @pl.when(owns_w)
+    def _():
+        wait_recv(part_land.at[pl.ds(0, HEADS - 1)], 12)
+
+    @pl.when(jnp.logical_not(owns_w))
+    def _():
+        wait_recv(part_land, 12)
+
     w_grad_ref[...] = jnp.sum(part_land[...].astype(F32), axis=0)
 
     wait_recv(col_land.at[0, pl.ds(0, N_SEQ - 1)], 15)
@@ -628,10 +666,19 @@
     wait_sent(sib_send, 8)
     wait_sent(dkv_send.at[pl.ds(0, HEADS - 1)], 9)
     wait_sent(dq_send.at[pl.ds(0, HEADS - 1)], 13)
-    wait_sent(w_send.at[pl.ds(0, N_TABLE - 1)], 10)
+    wait_sent(w_sib_send, 18)
+
+    @pl.when(owns_w)
+    def _():
+        wait_sent(w_send.at[pl.ds(0, 15)], 10)
+        wait_sent(w_land.at[pl.ds(0, N_SEQ - 1)], 12)
+
+    @pl.when(jnp.logical_not(owns_w))
+    def _():
+        wait_sent(w_send, 10)
+
     wait_sent(dx_send.at[pl.ds(0, 15)], 11)
     wait_sent(dx_send.at[pl.ds(0, 16)], 16)
-    wait_sent(part_land.at[pl.ds(0, N_SEQ - 1)], 12)
     wait_sent(col_send.at[0, pl.ds(0, N_SEQ - 1)], 15)
     wait_sent(col_send.at[1, pl.ds(0, N_SEQ - 1)], 17)
 
@@ -663,10 +710,13 @@
         buf((HEADS, 24, 128), F32),
         buf((HEADS, HEAD, 128), BF16),
         buf((HEADS, HEAD, 128), BF16),
-        buf((N_TABLE, 16, WIDTH), BF16),
+        buf((N_TABLE, 16, WIDTH), F32),
+        buf((16, 16, WIDTH), BF16),
+        buf((16, 16, WIDTH), BF16),
+        buf((16, 16, WIDTH), BF16),
         buf((N_TABLE, 16, WIDTH), BF16),
         buf((16, WIDTH), BF16),
-        buf((N_SEQ, 16, WIDTH), BF16),
+        buf((HEADS, 16, WIDTH), BF16),
         buf((HEADS, 128, 128), BF16),
         buf((HEADS, 128, 128), BF16),
         buf((HEADS, 128, 128), BF16),
@@ -695,8 +745,8 @@
         buf((8, N_SEQ * 32, 128), F32),
         buf((SLOTS, 128), F32),
         pltpu.SemaphoreType.DMA((5,)),
-        pltpu.SemaphoreType.DMA((18,)),
-        pltpu.SemaphoreType.DMA((18,)),
+        pltpu.SemaphoreType.DMA((19,)),
+        pltpu.SemaphoreType.DMA((19,)),
         pltpu.SemaphoreType.DMA((HEADS,)),
         pltpu.SemaphoreType.DMA((2,)),
     ]

time: 92.3 us -> 89.1 us (0.965)
  Pallas kernels: 89.6 us -> 86.5 us
    pallas_call x1, Pallas kernels: 89.6 us -> 86.5 us  [on_device(): pl.pallas_call(kernel, out_shape=(pltpu.VMEM((32, ROWS_T), F32), pltpu.VM...]
where the time goes in v4:
time: 89.1 us; the launch traced here: 89 us
  Pallas kernels  86.5 us (97%)
  between operations  1.28 us (1%)
  local copies, waits for them, and re-layouts  1.27 us (1%)
    pallas_call x1, Pallas kernels, on_device(): pl.pallas_call(kernel, out_shape=(pltpu.VMEM((32, ROWS_T), F32), pltpu.VM...  86.5 us

profile of v4, /device:TPU:1, one launch (start us, length us, event | category | flops | bytes accessed | tf_op | source)
XLA Modules:
  0.0 89.0 jit_solution(153404468528165992)
XLA Ops:
  1.3 86.5 %shard_map.77 = (f32[32,1024]{1,0:T(8,128)S(1)}, f32[16,512]{1,0:T(8,128)S(1)}) custom-call(s32[1,128]{1,0:T(1,128)} %rows_hbm.1, s32[1]{0:T(128)S(6)} %copy.12.len_ref, bf16[128,512]{1,0:T(8,128)(2,1)} %bitcast.3, bf16[1024,512]{1,0:T(8,128)(2,1)} %table_hbm.1, bf16[512,2048]{1,0:T(8,128)(2,1)} %w_in_hbm.1, bf16[512,512]{1,0:T(8,128)(2,1)} %w_out_hbm.1), custom_call_target="tpu_custom_call" | custom-call | tf_op jit(solution)/shard_map/pallas_call | solution.py:753
  87.7 0.7 copy.10
  88.4 0.6 copy.11

commit v5 on v4

--- a/solution.py
+++ b/solution.py
@@ -559,25 +559,27 @@
     def _():
         w_land[me_t] = w_send[me_t % 16]
 
+    place_t = one_hot(iota((SLOTS, EVENTS), 0) == slot_row)
+    wait_recv(dq_land.at[pl.ds(0, HEADS - 1)], 13)
+    d_q = dq_land[...].reshape(WIDTH, EVENTS).astype(F32).T
+    d_pre_q = (d_q * slope_s[:, 2 * WIDTH : 3 * WIDTH]).astype(BF16)
+    dn_q = dn_u + mm_t(d_pre_q, w_in_v[:, 2 * WIDTH : 3 * WIDTH])
     wait_recv(dkv_land.at[pl.ds(0, HEADS - 1)], 9)
-    wait_recv(dq_land.at[pl.ds(0, HEADS - 1)], 13)
-    d_k, d_v, d_q = [], [], []
+    d_k, d_v = [], []
     for p in range(4):
         first = dkv_land[2 * p].astype(F32)
         second = dkv_land[2 * p + 1].astype(F32)
         d_k.append(jnp.where(lane_e, first, swap(second)))
         d_v.append(jnp.where(lane_e, swap(first), second))
-        pair = [dq_land[2 * p + n].astype(F32) for n in range(2)]
-        d_q.append(jnp.concatenate(pair, axis=0).T)
-    d_proj = jnp.concatenate(d_v + d_q + d_k, axis=1)
-    d_pre = (d_proj * slope_s[:, WIDTH:]).astype(BF16)
-    dn = dn_u + mm_t(d_pre, w_in_v[:, WIDTH:])
+    d_pre_v = (jnp.concatenate(d_v, axis=1) * slope_s[:, WIDTH : 2 * WIDTH]).astype(BF16)
+    d_pre_k = (jnp.concatenate(d_k, axis=1) * slope_s[:, 3 * WIDTH :]).astype(BF16)
+    dn = dn_q + mm_t(d_pre_v, w_in_v[:, WIDTH : 2 * WIDTH])
+    dn = dn + mm_t(d_pre_k, w_in_v[:, 3 * WIDTH :])
     nx = nx_s[...]
     first = jnp.mean(dn, axis=1, keepdims=True)
     second = jnp.mean(dn * nx, axis=1, keepdims=True)
     d_x = grad_s[...] + rs1 * (dn - first - nx * second)
 
-    place_t = one_hot(iota((SLOTS, EVENTS), 0) == slot_row)
     dx_send[...] = stack_halves(mm(place_t, d_x.astype(BF16)))
     to_table_group(dx_send, dx_land, 11, 1)
     to_table_group(dx_send, dx_land, 16, 0)

time: 89.1 us -> 88.7 us (level)
  no operation moved by 1% of the time
where the time goes in v5:
time: 88.7 us; the launch traced here: 88.6 us
  Pallas kernels  86 us (97%)
  between operations  1.28 us (1%)
  local copies, waits for them, and re-layouts  1.27 us (1%)
    pallas_call x1, Pallas kernels, on_device(): pl.pallas_call(kernel, out_shape=(pltpu.VMEM((32, ROWS_T), F32), pltpu.VM...  86 us

profile of v5, /device:TPU:1, one launch (start us, length us, event | category | flops | bytes accessed | tf_op | source)
XLA Modules:
  0.0 88.6 jit_solution(12577617729288723033)
XLA Ops:
  1.3 86.0 %shard_map.77 = (f32[32,1024]{1,0:T(8,128)S(1)}, f32[16,512]{1,0:T(8,128)S(1)}) custom-call(s32[1,128]{1,0:T(1,128)} %rows_hbm.1, s32[1]{0:T(128)S(6)} %copy.12.len_ref, bf16[128,512]{1,0:T(8,128)(2,1)} %bitcast.3, bf16[1024,512]{1,0:T(8,128)(2,1)} %table_hbm.1, bf16[512,2048]{1,0:T(8,128)(2,1)} %w_in_hbm.1, bf16[512,512]{1,0:T(8,128)(2,1)} %w_out_hbm.1), custom_call_target="tpu_custom_call" | custom-call | tf_op jit(solution)/shard_map/pallas_call | solution.py:755
  87.3 0.7 copy.10
  88.0 0.6 copy.11
